TPU v7x, 512 devices: a whole 4x4x16 slice. The times are simulated.
512 devices in a mesh: seq: 64 (over y, z_lo, core), ch: 8 (over x, z_hi).
Axes of the slice: x: 4, y: 4, z: 16 (z_hi: 2, z_lo: 8; z = z_hi * 8 + z_lo), core: 2. Of those that a mesh axis runs over, the one named last changes fastest.
Arguments:
- query: bfloat16 [16384, 2048], P('seq', 'ch'), may hold values from -6 to 6
- key_proj: bfloat16 [16384, 2048], P('seq', 'ch'), may hold values from -6 to 6
- value: bfloat16 [16384, 2048], P('seq', 'ch'), may hold values from -6 to 6
- filt: float32 [16384, 2048], P('seq', 'ch'), may hold values from -0.046875 to 0.046875
- skip: float32 [2048], P('ch'), may hold values from 0.5 to 1.5
- cotangent: bfloat16 [16384, 2048], P('seq', 'ch'), may hold values from -6 to 6
- suffix_start: int32 [1], replicated, may hold values from 4096 to 8191
- layer_input: bfloat16 [16384, 2048], P('seq', 'ch'), may hold values from -2 to 2
- in_weight: bfloat16 [6144, 2048], P(None, 'ch'), may hold values from -0.078125 to 0.078125
Outputs:
- input_grad: bfloat16 [16384, 2048], P('seq', 'ch')
- attribution: float32 [16384], P('seq')
All inputs are finite; a program needn't handle non-finite values.
Results may differ from a plain program's by a relative error of at most 0.0049.
Values may be sent and summed in bfloat16 or wider, within the bound.
A program may use at most 64 MiB of HBM per device.

v0:
```python
import math

import jax
import jax.numpy as jnp
from jax import lax
from jax.sharding import PartitionSpec as P

N1 = 256


HIGHEST_PREC = lax.Precision.HIGHEST


def angle_table(first, second, modulus):
    product = first[:, None] * second[None, :] % modulus
    angles = 2.0 * math.pi / modulus * product.astype(jnp.float32)
    return (jnp.cos(angles), jnp.sin(angles))


def one_factor(count):
    return jnp.arange(count, dtype=jnp.int32)


def forward_spectrum(signal):
    parts = lax.axis_size("seq")
    place = lax.axis_index("seq")
    tokens, width = signal.shape
    rows = tokens // N1
    half = parts * rows
    full = 2 * half
    block = N1 // parts
    columns = lax.all_to_all(
        signal.reshape(rows, N1, width), "seq", split_axis=1, concat_axis=0, tiled=True
    )
    flat = columns.reshape(half, block * width)
    cos_two, sin_two = angle_table(one_factor(full), one_factor(half), full)
    real_part = jnp.dot(cos_two, flat, precision=HIGHEST_PREC).reshape(full, block, width)
    imag_part = -jnp.dot(sin_two, flat, precision=HIGHEST_PREC).reshape(full, block, width)
    first_index = place * block + one_factor(block)
    cos_turn, sin_turn = angle_table(one_factor(full), first_index, N1 * full)
    cos_turn = cos_turn[:, :, None]
    sin_turn = sin_turn[:, :, None]
    turned_real = real_part * cos_turn + imag_part * sin_turn
    turned_imag = imag_part * cos_turn - real_part * sin_turn
    spread_real, spread_imag = (
        lax.all_to_all(turned_real, "seq", split_axis=0, concat_axis=1, tiled=True),
        lax.all_to_all(turned_imag, "seq", split_axis=0, concat_axis=1, tiled=True),
    )
    cos_one, sin_one = angle_table(one_factor(N1), one_factor(N1), N1)
    out_real = jnp.einsum("kn,anw->akw", cos_one, spread_real, precision=HIGHEST_PREC) + jnp.einsum(
        "kn,anw->akw", sin_one, spread_imag, precision=HIGHEST_PREC
    )
    out_imag = jnp.einsum("kn,anw->akw", cos_one, spread_imag, precision=HIGHEST_PREC) - jnp.einsum(
        "kn,anw->akw", sin_one, spread_real, precision=HIGHEST_PREC
    )
    return (out_real, out_imag)


def first_inverse(spec_real, spec_imag):
    parts = lax.axis_size("seq")
    place = lax.axis_index("seq")
    kblock = spec_real.shape[0]
    full = kblock * parts
    cos_one, sin_one = angle_table(one_factor(N1), one_factor(N1), N1)
    back_real = jnp.einsum("kn,akw->anw", cos_one, spec_real, precision=HIGHEST_PREC) - jnp.einsum(
        "kn,akw->anw", sin_one, spec_imag, precision=HIGHEST_PREC
    )
    back_imag = jnp.einsum("kn,akw->anw", cos_one, spec_imag, precision=HIGHEST_PREC) + jnp.einsum(
        "kn,akw->anw", sin_one, spec_real, precision=HIGHEST_PREC
    )
    freq_index = place * kblock + one_factor(kblock)
    cos_turn, sin_turn = angle_table(freq_index, one_factor(N1), N1 * full)
    cos_turn = cos_turn[:, :, None]
    sin_turn = sin_turn[:, :, None]
    turned_real = back_real * cos_turn - back_imag * sin_turn
    turned_imag = back_imag * cos_turn + back_real * sin_turn
    return (turned_real, turned_imag)


def inverse_signal(spec_real, spec_imag):
    parts = lax.axis_size("seq")
    kblock, first_len, width = spec_real.shape
    full = kblock * parts
    half = full // 2
    block = N1 // parts
    turned_real, turned_imag = first_inverse(spec_real, spec_imag)
    gathered_real, gathered_imag = (
        lax.all_to_all(turned_real, "seq", split_axis=1, concat_axis=0, tiled=True),
        lax.all_to_all(turned_imag, "seq", split_axis=1, concat_axis=0, tiled=True),
    )
    cos_two, sin_two = angle_table(one_factor(half), one_factor(full), full)
    flat_real = gathered_real.reshape(full, block * width)
    flat_imag = gathered_imag.reshape(full, block * width)
    result = jnp.dot(cos_two, flat_real, precision=HIGHEST_PREC) - jnp.dot(
        sin_two, flat_imag, precision=HIGHEST_PREC
    )
    result = (result * (1.0 / (N1 * full))).reshape(half, block, width)
    rows_back = lax.all_to_all(result, "seq", split_axis=0, concat_axis=1, tiled=True)
    return rows_back.reshape(-1, width)


def shards(query, key_proj, value, filt, skip, cotangent, suffix_start, layer_input, in_weight):
    tokens, width = query.shape
    place = lax.axis_index("seq")
    positions = place * tokens + jnp.arange(tokens, dtype=jnp.int32)
    kept = (positions >= suffix_start[0]).astype(jnp.float32)[:, None]
    grad_out = cotangent.astype(jnp.float32) * kept
    key_vals = key_proj.astype(jnp.float32)
    value_vals = value.astype(jnp.float32)
    mixed = key_vals * value_vals
    grad_mixed_in = grad_out * query.astype(jnp.float32)
    spec_real, spec_imag = forward_spectrum(jnp.concatenate([mixed, filt], axis=1))
    mix_r = spec_real[:, :, :width]
    mix_i = spec_imag[:, :, :width]
    filt_r = spec_real[:, :, width:]
    filt_i = spec_imag[:, :, width:]
    adj_r, adj_i = forward_spectrum(grad_mixed_in)
    conv_r = filt_r * mix_r - filt_i * mix_i
    conv_i = filt_r * mix_i + filt_i * mix_r
    corr_r = filt_r * adj_r + filt_i * adj_i
    corr_i = filt_r * adj_i - filt_i * adj_r
    conv_out = inverse_signal(conv_r, conv_i)
    corr_out = inverse_signal(corr_r, corr_i)
    mixed_out = conv_out + skip[None, :] * mixed
    grad_query = grad_out * mixed_out
    grad_mixed = corr_out + skip[None, :] * grad_mixed_in
    grad_key = grad_mixed * value_vals
    grad_value = grad_mixed * key_vals
    stacked = (
        jnp.stack([grad_query, grad_key, grad_value], axis=0)
        .astype(jnp.bfloat16)
        .transpose(0, 2, 1)
    )
    features = in_weight.shape[1]
    weights = in_weight.reshape(3, in_weight.shape[0] // 3, features)
    full_grad = jnp.einsum(
        "jct,jcd->td",
        lax.all_gather(stacked, "ch", axis=1, tiled=True),
        weights,
        preferred_element_type=jnp.float32,
    )
    partial_score = jnp.sum(full_grad * layer_input.astype(jnp.float32), axis=1)
    attribution = lax.psum(partial_score, "ch")
    return (full_grad.astype(jnp.bfloat16), attribution)


def solution(mesh):
    in_specs = (
        P("seq", "ch"),
        P("seq", "ch"),
        P("seq", "ch"),
        P("seq", "ch"),
        P("ch"),
        P("seq", "ch"),
        P(),
        P("seq", "ch"),
        P(None, "ch"),
    )
    out_specs = (P("seq", "ch"), P("seq"))
    return jax.shard_map(shards, mesh=mesh, in_specs=in_specs, out_specs=out_specs, check_vma=False)
```

profile of v0, /device:TPU:200, one launch (start us, length us, event | category | flops | bytes accessed | tf_op | source)
XLA Modules:
  0.0 707.3 jit_solution(13294902002463591971)
XLA Ops:
  10.8 1.8 copy.82
  12.5 13.7 %all-to-all-start.6 = ((f32[1,256,256]{2,0,1:T(1,128)}), f32[1,256,256]{2,0,1:T(1,128)}, u32[]{:S(2)}, u32[]{:S(2)}) async-start(f32[1,256,256]{2,0,1:T(1,128)} %copy.82), calls=%async_computation.6 | async-start | bytes 524288 | tf_op jit(solution)/shard_map/all_to_all | solution.py:32
  27.3 1.9 copy.64
  31.7 1.8 maximum_bitcast_fusion
  33.5 1.9 copy.65
  35.4 3.7 all-to-all-done.6
  39.1 13.4 %all-to-all-start = ((f32[1,256,512]{2,0,1:T(1,128)}), f32[1,256,512]{2,0,1:T(1,128)}, u32[]{:S(2)}, u32[]{:S(2)}) async-start(f32[1,256,512]{2,0,1:T(1,128)} %copy.65), calls=%async_computation | async-start | bytes 1048576 | tf_op jit(solution)/shard_map/all_to_all | solution.py:32
  52.7 2.3 reduce.1
  59.5 16.4 %all-to-all-done = f32[1,256,512]{2,0,1:T(1,128)} async-done(((f32[1,256,512]{2,0,1:T(1,128)}), f32[1,256,512]{2,0,1:T(1,128)}, u32[]{:S(2)}, u32[]{:S(2)}) %all-to-all-start) | async-done | bytes 524320 | tf_op jit(solution)/shard_map/all_to_all | solution.py:32
  76.0 13.8 %all-to-all-start.8 = ((f32[128,4,256]{2,1,0:T(4,128)}), f32[128,4,256]{2,1,0:T(4,128)}, u32[]{:S(2)}, u32[]{:S(2)}) async-start(f32[128,4,256]{2,1,0:T(4,128)} %copy.88), calls=%async_computation.8 | async-start | bytes 1048576 | tf_op jit(solution)/shard_map/all_to_all | solution.py:47
  89.7 2.2 copy.85
  91.9 21.2 %all-to-all-done.8 = f32[128,4,256]{2,1,0:T(4,128)} async-done(((f32[128,4,256]{2,1,0:T(4,128)}), f32[128,4,256]{2,1,0:T(4,128)}, u32[]{:S(2)}, u32[]{:S(2)}) %all-to-all-start.8) | async-done | bytes 524320 | tf_op jit(solution)/shard_map/all_to_all | solution.py:47
  113.1 14.2 %all-to-all-start.7 = ((f32[128,4,256]{2,1,0:T(4,128)}), f32[128,4,256]{2,1,0:T(4,128)}, u32[]{:S(2)}, u32[]{:S(2)}) async-start(f32[128,4,256]{2,1,0:T(4,128)} %copy.85), calls=%async_computation.7 | async-start | bytes 1048576 | tf_op jit(solution)/shard_map/all_to_all | solution.py:46
  127.3 3.1 reduce
  130.4 2.1 reshape.191
  132.5 2.2 fusion.7
  134.7 3.4 multiply_add_fusion
  139.7 10.8 %all-to-all-done.7 = f32[128,4,256]{2,1,0:T(4,128)} async-done(((f32[128,4,256]{2,1,0:T(4,128)}), f32[128,4,256]{2,1,0:T(4,128)}, u32[]{:S(2)}, u32[]{:S(2)}) %all-to-all-start.7) | async-done | bytes 524320 | tf_op jit(solution)/shard_map/all_to_all | solution.py:46
  150.5 13.8 %all-to-all-start.2 = ((f32[128,4,512]{2,1,0:T(4,128)}), f32[128,4,512]{2,1,0:T(4,128)}, u32[]{:S(2)}, u32[]{:S(2)}) async-start(f32[128,4,512]{2,1,0:T(4,128)} %copy.71), calls=%async_computation.2 | async-start | bytes 2097152 | tf_op jit(solution)/shard_map/all_to_all | solution.py:47
  164.3 2.9 copy.68
  167.2 42.7 %all-to-all-done.2 = f32[128,4,512]{2,1,0:T(4,128)} async-done(((f32[128,4,512]{2,1,0:T(4,128)}), f32[128,4,512]{2,1,0:T(4,128)}, u32[]{:S(2)}, u32[]{:S(2)}) %all-to-all-start.2) | async-done | bytes 1048608 | tf_op jit(solution)/shard_map/all_to_all | solution.py:47
  209.8 14.6 %all-to-all-start.1 = ((f32[128,4,512]{2,1,0:T(4,128)}), f32[128,4,512]{2,1,0:T(4,128)}, u32[]{:S(2)}, u32[]{:S(2)}) async-start(f32[128,4,512]{2,1,0:T(4,128)} %copy.68), calls=%async_computation.1 | async-start | bytes 2097152 | tf_op jit(solution)/shard_map/all_to_all | solution.py:46
  224.6 2.1 copy.89
  226.7 2.0 copy.90
  228.8 2.1 copy.86
  230.9 2.0 copy.87
  232.9 2.6 fusion.31
  235.5 3.4 fusion.33
  238.9 3.4 fusion.2
  242.3 2.7 copy.72
  245.1 2.3 copy.73
  247.3 4.2 fusion.39
  251.5 18.3 %all-to-all-done.1 = f32[128,4,512]{2,1,0:T(4,128)} async-done(((f32[128,4,512]{2,1,0:T(4,128)}), f32[128,4,512]{2,1,0:T(4,128)}, u32[]{:S(2)}, u32[]{:S(2)}) %all-to-all-start.1) | async-done | bytes 1048608 | tf_op jit(solution)/shard_map/all_to_all | solution.py:46
  269.8 2.7 copy.69
  272.5 2.4 copy.70
  274.9 3.3 fusion.41
  278.2 3.7 fusion
  281.9 2.0 fusion.1
  288.8 1.8 convolution_add_fusion.3
  296.8 2.9 add_bitcast_fusion.1
  299.8 2.0 copy.93
  301.8 14.0 %all-to-all-start.9 = ((f32[2,256,256]{2,0,1:T(2,128)}), f32[2,256,256]{2,0,1:T(2,128)}, u32[]{:S(2)}, u32[]{:S(2)}) async-start(f32[2,256,256]{2,0,1:T(2,128)} %copy.93), calls=%async_computation.9 | async-start | bytes 1048576 | tf_op jit(solution)/shard_map/all_to_all | solution.py:88
  315.8 2.0 copy.95
  317.9 21.4 %all-to-all-done.9 = f32[2,256,256]{2,0,1:T(2,128)} async-done(((f32[2,256,256]{2,0,1:T(2,128)}), f32[2,256,256]{2,0,1:T(2,128)}, u32[]{:S(2)}, u32[]{:S(2)}) %all-to-all-start.9) | async-done | bytes 524320 | tf_op jit(solution)/shard_map/all_to_all | solution.py:88
  339.3 13.8 %all-to-all-start.10 = ((f32[2,256,256]{2,0,1:T(2,128)}), f32[2,256,256]{2,0,1:T(2,128)}, u32[]{:S(2)}, u32[]{:S(2)}) async-start(f32[2,256,256]{2,0,1:T(2,128)} %copy.95), calls=%async_computation.10 | async-start | bytes 1048576 | tf_op jit(solution)/shard_map/all_to_all | solution.py:89
  353.0 2.0 copy.76
  355.1 21.4 %all-to-all-done.10 = f32[2,256,256]{2,0,1:T(2,128)} async-done(((f32[2,256,256]{2,0,1:T(2,128)}), f32[2,256,256]{2,0,1:T(2,128)}, u32[]{:S(2)}, u32[]{:S(2)}) %all-to-all-start.10) | async-done | bytes 524320 | tf_op jit(solution)/shard_map/all_to_all | solution.py:89
  376.4 13.8 %all-to-all-start.3 = ((f32[2,256,256]{2,0,1:T(2,128)}), f32[2,256,256]{2,0,1:T(2,128)}, u32[]{:S(2)}, u32[]{:S(2)}) async-start(f32[2,256,256]{2,0,1:T(2,128)} %copy.76), calls=%async_computation.3 | async-start | bytes 1048576 | tf_op jit(solution)/shard_map/all_to_all | solution.py:88
  390.2 2.0 copy.78
  392.3 21.4 %all-to-all-done.3 = f32[2,256,256]{2,0,1:T(2,128)} async-done(((f32[2,256,256]{2,0,1:T(2,128)}), f32[2,256,256]{2,0,1:T(2,128)}, u32[]{:S(2)}, u32[]{:S(2)}) %all-to-all-start.3) | async-done | bytes 524320 | tf_op jit(solution)/shard_map/all_to_all | solution.py:88
  413.6 13.8 %all-to-all-start.4 = ((f32[2,256,256]{2,0,1:T(2,128)}), f32[2,256,256]{2,0,1:T(2,128)}, u32[]{:S(2)}, u32[]{:S(2)}) async-start(f32[2,256,256]{2,0,1:T(2,128)} %copy.78), calls=%async_computation.4 | async-start | bytes 1048576 | tf_op jit(solution)/shard_map/all_to_all | solution.py:89
  431.9 18.9 %all-to-all-done.4 = f32[2,256,256]{2,0,1:T(2,128)} async-done(((f32[2,256,256]{2,0,1:T(2,128)}), f32[2,256,256]{2,0,1:T(2,128)}, u32[]{:S(2)}, u32[]{:S(2)}) %all-to-all-start.4) | async-done | bytes 524320 | tf_op jit(solution)/shard_map/all_to_all | solution.py:89
  450.8 13.8 %all-to-all-start.11 = ((f32[64,4,256]{2,1,0:T(4,128)}), f32[64,4,256]{2,1,0:T(4,128)}, u32[]{:S(2)}, u32[]{:S(2)}) async-start(f32[64,4,256]{2,1,0:T(4,128)} %reshape.200), calls=%async_computation.11 | async-start | bytes 524288 | tf_op jit(solution)/shard_map/all_to_all | solution.py:98
  469.0 1.8 reshape.194
  470.8 6.7 all-to-all-done.11
  477.5 13.4 %all-to-all-start.5 = ((f32[64,4,256]{2,1,0:T(4,128)}), f32[64,4,256]{2,1,0:T(4,128)}, u32[]{:S(2)}, u32[]{:S(2)}) async-start(f32[64,4,256]{2,1,0:T(4,128)} %reshape.194), calls=%async_computation.5 | async-start | bytes 524288 | tf_op jit(solution)/shard_map/all_to_all | solution.py:98
  490.9 1.8 reshape.201
  492.7 1.8 copy.97
  494.4 9.3 %all-to-all-done.5 = f32[64,4,256]{2,1,0:T(4,128)} async-done(((f32[64,4,256]{2,1,0:T(4,128)}), f32[64,4,256]{2,1,0:T(4,128)}, u32[]{:S(2)}, u32[]{:S(2)}) %all-to-all-start.5) | async-done | bytes 262176 | tf_op jit(solution)/shard_map/all_to_all | solution.py:98
  503.8 1.8 reshape.195
  505.5 1.8 copy.80
  510.4 142.7 %all-gather.2.cloned.1.call-done = bf16[3,2048,256]{2,1,0:T(8,128)(2,1)} async-done(((bf16[3,256,256]{2,1,0:T(8,128)(2,1)}), bf16[3,2048,256]{2,1,0:T(8,128)(2,1)}) %all-gather.2.cloned.1.call-update) | async-done | bytes 3145744 | tf_op jit(solution)/shard_map/all_gather | solution.py:138
  653.1 3.2 multiply_reduce_fusion
  657.1 43.0 %psum.7 = f32[256]{0:T(256)} all-reduce(f32[256]{0:T(256)S(1)} %get-tuple-element.25), channel_id=1, replica_groups=mesh['seq'=64,'ch'=8] {'ch'}, use_global_device_ids=true, to_apply=%region_1.2 | all-reduce | flops 256 | bytes 2048 | tf_op jit(solution)/shard_map/psum | solution.py:143
  (62 shorter events, 36.8 us)
Async XLA Ops:
  7.2 645.9 %copy-start = (bf16[6144,256]{1,0:T(8,128)(2,1)S(1)}, bf16[6144,256]{1,0:T(8,128)(2,1)}, u32[]{:S(2)}) copy-start(bf16[6144,256]{1,0:T(8,128)(2,1)} %param.17) | copy-start | bytes 9437188
  9.4 29.8 %copy-start.4 = (bf16[256,256]{0,1:T(8,128)(2,1)}, bf16[256,256]{0,1:T(8,128)(2,1)S(1)}, u32[]{:S(2)}) copy-start(bf16[256,256]{0,1:T(8,128)(2,1)S(1)} %copy.61) | copy-start | bytes 393220
  12.5 26.6 %all-to-all-start.6 = ((f32[1,256,256]{2,0,1:T(1,128)}), f32[1,256,256]{2,0,1:T(1,128)}, u32[]{:S(2)}, u32[]{:S(2)}) async-start(f32[1,256,256]{2,0,1:T(1,128)} %copy.82), calls=%async_computation.6 | async-start | bytes 524288 | tf_op jit(solution)/shard_map/all_to_all | solution.py:32
  27.3 25.4 %copy-start.6 = (bf16[256,256]{0,1:T(8,128)(2,1)}, bf16[256,256]{0,1:T(8,128)(2,1)S(1)}, u32[]{:S(2)}) copy-start(bf16[256,256]{0,1:T(8,128)(2,1)S(1)} %copy.63) | copy-start | bytes 393220
  39.1 36.8 %all-to-all-start = ((f32[1,256,512]{2,0,1:T(1,128)}), f32[1,256,512]{2,0,1:T(1,128)}, u32[]{:S(2)}, u32[]{:S(2)}) async-start(f32[1,256,512]{2,0,1:T(1,128)} %copy.65), calls=%async_computation | async-start | bytes 1048576 | tf_op jit(solution)/shard_map/all_to_all | solution.py:32
  76.0 37.2 %all-to-all-start.8 = ((f32[128,4,256]{2,1,0:T(4,128)}), f32[128,4,256]{2,1,0:T(4,128)}, u32[]{:S(2)}, u32[]{:S(2)}) async-start(f32[128,4,256]{2,1,0:T(4,128)} %copy.88), calls=%async_computation.8 | async-start | bytes 1048576 | tf_op jit(solution)/shard_map/all_to_all | solution.py:47
  113.1 37.4 %all-to-all-start.7 = ((f32[128,4,256]{2,1,0:T(4,128)}), f32[128,4,256]{2,1,0:T(4,128)}, u32[]{:S(2)}, u32[]{:S(2)}) async-start(f32[128,4,256]{2,1,0:T(4,128)} %copy.85), calls=%async_computation.7 | async-start | bytes 1048576 | tf_op jit(solution)/shard_map/all_to_all | solution.py:46
  150.5 59.3 %all-to-all-start.2 = ((f32[128,4,512]{2,1,0:T(4,128)}), f32[128,4,512]{2,1,0:T(4,128)}, u32[]{:S(2)}, u32[]{:S(2)}) async-start(f32[128,4,512]{2,1,0:T(4,128)} %copy.71), calls=%async_computation.2 | async-start | bytes 2097152 | tf_op jit(solution)/shard_map/all_to_all | solution.py:47
  209.8 60.0 %all-to-all-start.1 = ((f32[128,4,512]{2,1,0:T(4,128)}), f32[128,4,512]{2,1,0:T(4,128)}, u32[]{:S(2)}, u32[]{:S(2)}) async-start(f32[128,4,512]{2,1,0:T(4,128)} %copy.68), calls=%async_computation.1 | async-start | bytes 2097152 | tf_op jit(solution)/shard_map/all_to_all | solution.py:46
  274.9 7.0 copy-start.1
  278.2 5.7 copy-start.2
  278.2 5.7 copy-start.3
  278.2 5.7 copy-start.8
  301.8 37.4 %all-to-all-start.9 = ((f32[2,256,256]{2,0,1:T(2,128)}), f32[2,256,256]{2,0,1:T(2,128)}, u32[]{:S(2)}, u32[]{:S(2)}) async-start(f32[2,256,256]{2,0,1:T(2,128)} %copy.93), calls=%async_computation.9 | async-start | bytes 1048576 | tf_op jit(solution)/shard_map/all_to_all | solution.py:88
  339.3 37.2 %all-to-all-start.10 = ((f32[2,256,256]{2,0,1:T(2,128)}), f32[2,256,256]{2,0,1:T(2,128)}, u32[]{:S(2)}, u32[]{:S(2)}) async-start(f32[2,256,256]{2,0,1:T(2,128)} %copy.95), calls=%async_computation.10 | async-start | bytes 1048576 | tf_op jit(solution)/shard_map/all_to_all | solution.py:89
  376.4 37.2 %all-to-all-start.3 = ((f32[2,256,256]{2,0,1:T(2,128)}), f32[2,256,256]{2,0,1:T(2,128)}, u32[]{:S(2)}, u32[]{:S(2)}) async-start(f32[2,256,256]{2,0,1:T(2,128)} %copy.76), calls=%async_computation.3 | async-start | bytes 1048576 | tf_op jit(solution)/shard_map/all_to_all | solution.py:88
  413.6 37.2 %all-to-all-start.4 = ((f32[2,256,256]{2,0,1:T(2,128)}), f32[2,256,256]{2,0,1:T(2,128)}, u32[]{:S(2)}, u32[]{:S(2)}) async-start(f32[2,256,256]{2,0,1:T(2,128)} %copy.78), calls=%async_computation.4 | async-start | bytes 1048576 | tf_op jit(solution)/shard_map/all_to_all | solution.py:89
  450.8 26.7 %all-to-all-start.11 = ((f32[64,4,256]{2,1,0:T(4,128)}), f32[64,4,256]{2,1,0:T(4,128)}, u32[]{:S(2)}, u32[]{:S(2)}) async-start(f32[64,4,256]{2,1,0:T(4,128)} %reshape.200), calls=%async_computation.11 | async-start | bytes 524288 | tf_op jit(solution)/shard_map/all_to_all | solution.py:98
  467.0 40.3 %copy-start.5 = (bf16[256,256]{0,1:T(8,128)(2,1)S(1)}, bf16[256,256]{0,1:T(8,128)(2,1)}, u32[]{:S(2)}) copy-start(bf16[256,256]{0,1:T(8,128)(2,1)} %copy-done.4) | copy-start | bytes 393220
  467.1 40.3 %copy-start.7 = (bf16[256,256]{0,1:T(8,128)(2,1)S(1)}, bf16[256,256]{0,1:T(8,128)(2,1)}, u32[]{:S(2)}) copy-start(bf16[256,256]{0,1:T(8,128)(2,1)} %copy-done.6) | copy-start | bytes 393220
  467.1 40.3 %copy-start.9 = (f32[256]{0:T(256)S(1)}, f32[256]{0:T(256)}, u32[]{:S(2)}) copy-start(f32[256]{0:T(256)} %param.13) | copy-start | bytes 3076
  477.5 26.3 %all-to-all-start.5 = ((f32[64,4,256]{2,1,0:T(4,128)}), f32[64,4,256]{2,1,0:T(4,128)}, u32[]{:S(2)}, u32[]{:S(2)}) async-start(f32[64,4,256]{2,1,0:T(4,128)} %reshape.194), calls=%async_computation.5 | async-start | bytes 524288 | tf_op jit(solution)/shard_map/all_to_all | solution.py:98
  490.9 162.2 %all-gather.2.cloned.1.call-start = ((), (), s32[]{:S(2)}) async-start(), calls=%async_computation.12 | async-start | bytes 3538944 | tf_op jit(solution)/shard_map/all_gather | solution.py:138
Sparse Core Ops, SparseCore 0:
  509.5 143.5 all-gather.1
where the time goes:
time: 716 us; the launch traced here: 707 us
  waiting for transfers between devices  355 us (50%)
  starting transfers between devices  166 us (23%)
  local copies, waits for them, and re-layouts  64.5 us (9%)
  matrix products  52.4 us (7%)
  blocking collectives  43 us (6%)
  between operations  15.6 us (2%)
  other arithmetic  11.1 us (2%)
    all_gather x1, waiting for transfers between devices, shards(): lax.all_gather(stacked, 'ch', axis=1, tiled=True)  143 us
    all_to_all x2, waiting for transfers between devices, forward_spectrum(): lax.all_to_all(turned_imag, 'seq', split_axis=0, concat_axis=1, tiled=True)  63.9 us
    psum x1, blocking collectives, shards(): attribution = lax.psum(partial_score, 'ch')  43 us
    all_to_all x2, waiting for transfers between devices, inverse_signal(): lax.all_to_all(turned_real, 'seq', split_axis=1, concat_axis=0, tiled=True)  42.7 us
    all_to_all x2, waiting for transfers between devices, inverse_signal(): lax.all_to_all(turned_imag, 'seq', split_axis=1, concat_axis=0, tiled=True)  40.3 us
    all_to_all x2, waiting for transfers between devices, forward_spectrum(): lax.all_to_all(turned_real, 'seq', split_axis=0, concat_axis=1, tiled=True)  29.1 us
    all_to_all x2, starting transfers between devices, forward_spectrum(): lax.all_to_all(turned_real, 'seq', split_axis=0, concat_axis=1, tiled=True)  28.8 us
    all_to_all x2, starting transfers between devices, inverse_signal(): lax.all_to_all(turned_real, 'seq', split_axis=1, concat_axis=0, tiled=True)  27.8 us
  transfers between devices with their start and end apart: 13, of which 13 were waited for; matrix products, arithmetic and copies ran while one was open for 12% of the time, Pallas kernels for 0%

commit v1 on v0

v1 whole, which is shorter than its diff:
```python
import functools

import jax
import jax.numpy as jnp
import numpy as np
from jax import lax
from jax.experimental import pallas as pl
from jax.experimental.pallas import tpu as pltpu
from jax.sharding import PartitionSpec as P

BF16 = jnp.bfloat16
F32 = jnp.float32
MESH = pl.DeviceIdType.MESH
LANES = 128
GROUP = 8


def split_high_low(table):
    high = table.astype(np.float32).astype(BF16)
    low = (table - high.astype(np.float64)).astype(np.float32).astype(BF16)
    return high, low


def transform_tables(sources, tokens):
    chips = sources // 2
    order = np.arange(sources)
    place = 2 * (order % chips) + order // chips
    odd = np.arange(sources) + 0.5
    angle_one = 2.0 * np.pi / (2 * sources) * (odd[:, None] * place[None, :])
    first = np.concatenate([np.cos(angle_one), -np.sin(angle_one)], axis=0)
    length = 2 * sources * tokens
    turn = 2.0 * np.pi / length * (odd[:, None] * np.arange(tokens)[None, :])
    angle_two = 2.0 * np.pi / tokens * (np.arange(tokens)[:, None] * np.arange(tokens)[None, :] % tokens)
    cos_two, sin_two = np.cos(angle_two), np.sin(angle_two)
    second = np.block([[cos_two, -sin_two], [sin_two, cos_two]])
    back = first.T * (2.0 / length)
    tables = []
    tables += split_high_low(first)
    tables += split_high_low(second)
    tables += split_high_low(second.T)
    tables += split_high_low(back)
    tables += [np.cos(turn).astype(np.float32), np.sin(turn).astype(np.float32)]
    return tables


def halves(array):
    high = array.astype(BF16)
    return high, (array - high.astype(F32)).astype(BF16)


def dot(left, right):
    return jnp.dot(left, right, preferred_element_type=F32)


def to_blocks(signal, chips):
    turned = signal.T
    left = turned[:, :LANES].reshape(chips, GROUP, LANES)
    right = turned[:, LANES:].reshape(chips, GROUP, LANES)
    return jnp.concatenate([left, right], axis=1).astype(BF16)


def from_blocks(blocks, chips):
    blocks = blocks.astype(F32)
    left = blocks[:, :GROUP].reshape(chips * GROUP, LANES)
    right = blocks[:, GROUP:].reshape(chips * GROUP, LANES)
    return jnp.concatenate([left.T, right.T], axis=0)


def conv_kernel(
    chips,
    query, key_proj, value, filt, cotangent, skip, suffix_start,
    one_hi, one_lo, two_hi, two_lo, inv_hi, inv_lo, back_hi, back_lo, turn_cos, turn_sin,
    grads,
    send, recv, rows_f32, flat, spec_hi, spec_lo, spec, time_hi, time_lo, results, outgoing, returned,
    send_sem, recv_sem, pair_sem, send_back_sem, recv_back_sem, pair_back_sem,
):
    sources = 2 * chips
    tokens, width = query.shape
    me = lax.axis_index("seq")
    chip = me // 2
    core = lax.rem(me, 2)
    partner = 2 * chip + (1 - core)

    def peer(step):
        return lax.rem(chip + step, chips)

    barrier = pltpu.get_barrier_semaphore()

    def greet(step, carry):
        pl.semaphore_signal(barrier, inc=1, device_id={"seq": 2 * peer(step) + core}, device_id_type=MESH)
        return carry

    lax.fori_loop(1, chips, greet, 0)
    pl.semaphore_signal(barrier, inc=1, device_id={"seq": partner}, device_id_type=MESH)

    keys = key_proj[...].astype(F32)
    values = value[...].astype(F32)
    mixed = keys * values
    positions = me * tokens + lax.broadcasted_iota(jnp.int32, (tokens, width), 0)
    grad_out = jnp.where(positions >= suffix_start[0], cotangent[...].astype(F32), 0.0)
    grad_mixed_in = grad_out * query[...].astype(F32)
    send[:, 0:16, :] = to_blocks(mixed, chips)
    send[:, 16:32, :] = to_blocks(filt[...], chips)
    send[:, 32:48, :] = to_blocks(grad_mixed_in, chips)

    pl.semaphore_wait(barrier, chips)

    def forward(step, index):
        return pltpu.make_async_remote_copy(
            src_ref=send.at[peer(step)],
            dst_ref=recv.at[core, index],
            send_sem=send_sem.at[step],
            recv_sem=recv_sem.at[index],
            device_id={"seq": 2 * peer(step) + core},
            device_id_type=MESH,
        )

    def start_forward(step, carry):
        forward(step, chip).start()
        return carry

    lax.fori_loop(1, chips, start_forward, 0)
    recv[core, chip] = send[chip]

    def end_forward(step, carry):
        copy = forward(step, peer(step))
        copy.wait_recv()
        copy.wait_send()
        return carry

    lax.fori_loop(1, chips, end_forward, 0)

    theirs = pl.ds(pl.multiple_of(16 * (1 - core), 16), 32)
    swap = pltpu.make_async_remote_copy(
        src_ref=recv.at[core, :, theirs],
        dst_ref=recv.at[core, :, theirs],
        send_sem=pair_sem.at[0],
        recv_sem=pair_sem.at[1],
        device_id={"seq": partner},
        device_id_type=MESH,
    )
    swap.start()
    swap.wait()

    sign = jnp.where(core == 0, 1.0, -1.0).astype(F32)
    for signal in range(2):
        if signal == 0:
            rows = recv[:, :, 16:32, :]
        else:
            rows = recv[:, :, pl.ds(pl.multiple_of(32 * core, 16), 16), :]
        rows_f32[...] = rows.astype(F32).reshape(sources * 16, LANES)
        for r in range(16):
            flat[:, r * LANES : (r + 1) * LANES] = rows_f32[pl.ds(r, sources, stride=16), :].astype(BF16)
        one = dot(one_hi[...], flat[...]) + dot(one_lo[...], flat[...])
        for r in range(16):
            half, channel = r // GROUP, r % GROUP
            columns = slice(half * LANES, (half + 1) * LANES)
            real = one[:sources, r * LANES : (r + 1) * LANES]
            imag = one[sources:, r * LANES : (r + 1) * LANES]
            cos, sin = turn_cos[:, columns], turn_sin[:, columns]
            place = slice((signal * GROUP + channel) * sources, (signal * GROUP + channel + 1) * sources)
            spec_hi[place, columns], spec_lo[place, columns] = halves(real * cos + imag * sin)
            columns = slice(tokens + half * LANES, tokens + (half + 1) * LANES)
            spec_hi[place, columns], spec_lo[place, columns] = halves(imag * cos - real * sin)
    spec[...] = (
        dot(spec_hi[...], two_hi[...]) + dot(spec_lo[...], two_hi[...]) + dot(spec_hi[...], two_lo[...])
    )
    count = GROUP * sources
    fr, fi = spec[:count, :tokens], spec[:count, tokens:] * sign
    pr, pi = spec[count:, :tokens], spec[count:, tokens:]
    product = jnp.concatenate([fr * pr - fi * pi, fr * pi + fi * pr], axis=1)
    prod_hi, prod_lo = halves(product)
    inverse = dot(prod_hi, inv_hi[...]) + dot(prod_lo, inv_hi[...]) + dot(prod_hi, inv_lo[...])
    for r in range(16):
        half, channel = r // GROUP, r % GROUP
        columns = slice(half * LANES, (half + 1) * LANES)
        place = slice(channel * sources, (channel + 1) * sources)
        real = inverse[place, columns]
        imag = inverse[place, tokens + half * LANES : tokens + (half + 1) * LANES]
        cos, sin = turn_cos[:, columns], turn_sin[:, columns]
        columns = slice(r * LANES, (r + 1) * LANES)
        time_hi[:sources, columns], time_lo[:sources, columns] = halves(real * cos - imag * sin)
        time_hi[sources:, columns], time_lo[sources:, columns] = halves(imag * cos + real * sin)
    result = dot(back_hi[...], time_hi[...]) + dot(back_lo[...], time_hi[...]) + dot(back_hi[...], time_lo[...])
    for r in range(16):
        rows_f32[pl.ds(r, sources, stride=16), :] = result[:, r * LANES : (r + 1) * LANES]
    results[...] = rows_f32[...].reshape(2, chips, 16, LANES).astype(BF16)

    mine = pl.ds(pl.multiple_of(16 * core, 16), 16)
    swap_back = pltpu.make_async_remote_copy(
        src_ref=results.at[1 - core],
        dst_ref=outgoing.at[:, mine],
        send_sem=pair_back_sem.at[0],
        recv_sem=pair_back_sem.at[1],
        device_id={"seq": partner},
        device_id_type=MESH,
    )
    swap_back.start()
    outgoing[:, mine, :] = results[core]
    swap_back.wait()

    def backward(step, index):
        return pltpu.make_async_remote_copy(
            src_ref=outgoing.at[peer(step)],
            dst_ref=returned.at[index],
            send_sem=send_back_sem.at[step],
            recv_sem=recv_back_sem.at[index],
            device_id={"seq": 2 * peer(step) + core},
            device_id_type=MESH,
        )

    def start_backward(step, carry):
        backward(step, chip).start()
        return carry

    lax.fori_loop(1, chips, start_backward, 0)
    returned[chip] = outgoing[chip]

    def end_backward(step, carry):
        copy = backward(step, peer(step))
        copy.wait_recv()
        copy.wait_send()
        return carry

    lax.fori_loop(1, chips, end_backward, 0)

    keys = key_proj[...].astype(F32)
    values = value[...].astype(F32)
    gains = skip[...]
    positions = me * tokens + lax.broadcasted_iota(jnp.int32, (tokens, width), 0)
    grad_out = jnp.where(positions >= suffix_start[0], cotangent[...].astype(F32), 0.0)
    conv_out = from_blocks(returned[:, 0:16, :], chips)
    grads[:, :width] = (grad_out * (conv_out + gains * (keys * values))).astype(BF16)
    grad_mixed_in = grad_out * query[...].astype(F32)
    grad_mixed = from_blocks(returned[:, 16:32, :], chips) + gains * grad_mixed_in
    grads[:, width : 2 * width] = (grad_mixed * values).astype(BF16)
    grads[:, 2 * width :] = (grad_mixed * keys).astype(BF16)


def projection_grads(query, key_proj, value, filt, cotangent, skip, suffix_start):
    tokens, width = query.shape
    sources = lax.axis_size("seq")
    chips = sources // 2
    tables = transform_tables(sources, tokens)
    vmem = pl.BlockSpec(memory_space=pltpu.VMEM)
    smem = pl.BlockSpec(memory_space=pltpu.SMEM)
    count = GROUP * sources
    return pl.pallas_call(
        functools.partial(conv_kernel, chips),
        out_shape=jax.ShapeDtypeStruct((tokens, 3 * width), BF16),
        in_specs=[vmem] * 6 + [smem] + [vmem] * len(tables),
        out_specs=vmem,
        scratch_shapes=[
            pltpu.VMEM((chips, 48, LANES), BF16),
            pltpu.VMEM((2, chips, 48, LANES), BF16),
            pltpu.VMEM((sources * 16, LANES), F32),
            pltpu.VMEM((sources, 16 * LANES), BF16),
            pltpu.VMEM((2 * count, 2 * tokens), BF16),
            pltpu.VMEM((2 * count, 2 * tokens), BF16),
            pltpu.VMEM((2 * count, 2 * tokens), F32),
            pltpu.VMEM((2 * sources, 16 * LANES), BF16),
            pltpu.VMEM((2 * sources, 16 * LANES), BF16),
            pltpu.VMEM((2, chips, 16, LANES), BF16),
            pltpu.VMEM((chips, 32, LANES), BF16),
            pltpu.VMEM((chips, 32, LANES), BF16),
            pltpu.SemaphoreType.DMA((chips,)),
            pltpu.SemaphoreType.DMA((chips,)),
            pltpu.SemaphoreType.DMA((2,)),
            pltpu.SemaphoreType.DMA((chips,)),
            pltpu.SemaphoreType.DMA((chips,)),
            pltpu.SemaphoreType.DMA((2,)),
        ],
        compiler_params=pltpu.CompilerParams(
            collective_id=0, has_side_effects=True, vmem_limit_bytes=48 * 1024 * 1024
        ),
        name="conv_grads",
    )(query, key_proj, value, filt, cotangent, skip, suffix_start, *[jnp.asarray(t) for t in tables])


def shards(query, key_proj, value, filt, skip, cotangent, suffix_start, layer_input, in_weight):
    tokens, width = query.shape
    grads = projection_grads(query, key_proj, value, filt, cotangent, skip[None, :], suffix_start)
    features = in_weight.shape[1]
    weights = in_weight.reshape(3, in_weight.shape[0] // 3, features)
    gathered = lax.all_gather(grads, "ch", axis=0)
    gathered = gathered.reshape(-1, tokens, 3, width)
    full_grad = jnp.einsum(
        "atjc,jacd->td",
        gathered,
        weights.reshape(3, -1, width, features),
        preferred_element_type=F32,
    )
    partial_score = jnp.sum(full_grad * layer_input.astype(F32), axis=1)
    attribution = lax.psum(partial_score, "ch")
    return full_grad.astype(BF16), attribution


def solution(mesh):
    in_specs = (
        P("seq", "ch"),
        P("seq", "ch"),
        P("seq", "ch"),
        P("seq", "ch"),
        P("ch"),
        P("seq", "ch"),
        P(),
        P("seq", "ch"),
        P(None, "ch"),
    )
    out_specs = (P("seq", "ch"), P("seq"))
    return jax.shard_map(shards, mesh=mesh, in_specs=in_specs, out_specs=out_specs, check_vma=False)
```

time: 716 us -> 286 us (0.40)
  the two profiles are of different devices: /device:TPU:200 before, /device:TPU:160 now
where the time goes in v1:
time: 286 us; the launch traced here: 285 us
  waiting for transfers between devices  145 us (51%)
  Pallas kernels  50.2 us (18%)
  blocking collectives  40.5 us (14%)
  local copies, waits for them, and re-layouts  29.9 us (10%)
  between operations  14.9 us (5%)
  matrix products  4.64 us (2%)
    all_gather x1, waiting for transfers between devices, shards(): gathered = lax.all_gather(grads, 'ch', axis=0)  145 us
    pallas_call x1, Pallas kernels, projection_grads(): pl.pallas_call(functools.partial(conv_kernel, chips), out_shape=jax.Shape...  50.2 us
    psum x1, blocking collectives, shards(): attribution = lax.psum(partial_score, 'ch')  40.5 us
    unnamed x38, local copies, waits for them, and re-layouts  15 us
    reshape x2, local copies, waits for them, and re-layouts, shards(): gathered = gathered.reshape(-1, tokens, 3, width)  14.9 us
  transfers between devices with their start and end apart: 1, of which 1 were waited for; matrix products, arithmetic and copies ran while one was open for 0% of the time, Pallas kernels for 0%

profile of v1, /device:TPU:160, one launch (start us, length us, event | category | flops | bytes accessed | tf_op | source)
XLA Modules:
  0.0 284.9 jit_solution(13819040964338657531)
XLA Ops:
  7.2 0.0 copy-start
  7.2 0.0 all-gather.3.cloned.1.call-start
  8.0 0.0 copy-start.1
  8.0 1.1 copy-done.1
  9.2 0.0 copy-start.2
  9.2 1.0 copy-done.2
  10.2 0.0 copy-start.3
  10.2 1.0 copy-done.3
  11.3 0.0 copy-start.4
  11.3 1.0 copy-done.4
  12.3 0.0 copy-start.5
  12.3 0.9 copy-done.5
  13.3 0.0 copy-start.6
  13.3 0.9 copy-done.6
  14.2 0.0 copy-start.7
  14.2 0.9 copy-done.7
  15.1 0.0 copy-start.8
  15.1 0.9 copy-done.8
  16.0 0.0 copy-start.9
  16.0 0.9 copy-done.9
  16.9 0.0 copy-start.10
  16.9 0.8 copy-done.10
  17.7 0.0 copy-start.11
  17.7 0.8 copy-done.11
  18.6 0.0 copy-start.12
  18.6 0.8 copy-done.12
  19.3 0.0 copy-start.13
  19.3 0.8 copy-done.13
  20.1 0.0 copy-start.14
  20.1 0.7 copy-done.14
  20.8 0.0 copy-start.15
  20.8 0.7 copy-done.15
  21.5 0.0 copy-start.16
  21.5 0.7 copy-done.16
  22.2 0.0 copy-start.17
  22.2 50.2 %conv_grads.1 = bf16[256,768]{1,0:T(8,128)(2,1)} custom-call(bf16[256,256]{1,0:T(8,128)(2,1)S(1)} %copy-done.6, bf16[256,256]{1,0:T(8,128)(2,1)S(1)} %copy-done.7, bf16[256,256]{1,0:T(8,128)(2,1)S(1)} %copy-done.8, f32[256,256]{1,0:T(8,128)S(1)} %copy-done.5, bf16[256,256]{1,0:T(8,128)(2,1)S(1)} %copy-done.9, f32[1,256]{1,0:T(1,128)S(1)} %bitcast.8, ...), custom_call_target="tpu_custom_call" | custom-call | tf_op jit(solution)/shard_map/conv_grads/pallas_call | solution.py:248
  72.4 0.0 all-gather.3.cloned.1.call-update
  72.4 0.0 copy-done.17
  72.4 0.1 copy.28
  72.5 144.7 %all-gather.3.cloned.1.call-done = bf16[2048,768]{1,0:T(8,128)(2,1)} async-done(((bf16[256,768]{1,0:T(8,128)(2,1)}), bf16[2048,768]{1,0:T(8,128)(2,1)}) %all-gather.3.cloned.1.call-update) | async-done | bytes 3145744 | tf_op jit(solution)/shard_map/all_gather | solution.py:285
  217.3 9.4 %reshape.11 = bf16[8,256,3,256]{3,2,1,0:T(4,128)(2,1)} reshape(bf16[2048,768]{1,0:T(8,128)(2,1)} %all-gather.3.cloned.1.call-done) | data formatting | bytes 6291456 | tf_op jit(solution)/shard_map/reshape | solution.py:286
  226.6 5.5 %copy.30 = bf16[8,256,3,256]{1,0,2,3:T(8,128)(2,1)} copy(bf16[8,256,3,256]{3,2,1,0:T(4,128)(2,1)} %reshape.11) | data formatting | bytes 6291456 | tf_op jit(solution)/shard_map/reshape | solution.py:286
  232.2 0.0 copy-done
  232.2 4.6 %multiply_reduce_fusion = (f32[256]{0:T(256)S(1)}, bf16[256,256]{0,1:T(8,128)(2,1)S(1)}) fusion(bf16[256,256]{0,1:T(8,128)(2,1)S(1)} %copy.28, bf16[8,256,3,256]{1,0,2,3:T(8,128)(2,1)} %copy.30, bf16[3,8,256,256]{3,2,1,0:T(8,128)(2,1)S(1)} %bitcast.7), kind=kOutput, calls=%fused_computation.3 | convolution fusion | flops 805568256 | bytes 6554624 | tf_op jit(solution)/shard_map/atjc,jacd->td/dot_general | solution.py:287
  236.8 0.8 copy.29
  237.6 40.5 %psum.7 = f32[256]{0:T(256)} all-reduce(f32[256]{0:T(256)S(1)} %get-tuple-element.6), channel_id=1, replica_groups=mesh['seq'=64,'ch'=8] {'ch'}, use_global_device_ids=true, to_apply=%region_1.0 | all-reduce | flops 256 | bytes 2048 | tf_op jit(solution)/shard_map/psum | solution.py:294
Async XLA Ops:
  7.2 225.0 %copy-start = (bf16[6144,256]{1,0:T(8,128)(2,1)S(1)}, bf16[6144,256]{1,0:T(8,128)(2,1)}, u32[]{:S(2)}) copy-start(bf16[6144,256]{1,0:T(8,128)(2,1)} %param.27) | copy-start | bytes 9437188
  7.2 210.1 %all-gather.3.cloned.1.call-start = ((), (), s32[]{:S(2)}) async-start(), calls=%async_computation | async-start | bytes 3538944 | tf_op jit(solution)/shard_map/all_gather | solution.py:285
  8.0 1.2 copy-start.1
  9.2 1.0 copy-start.2
  10.2 1.0 copy-start.3
  11.3 1.0 copy-start.4
  12.3 0.9 copy-start.5
  13.3 0.9 copy-start.6
  14.2 0.9 copy-start.7
  15.1 0.9 copy-start.8
  16.0 0.9 copy-start.9
  16.9 0.8 copy-start.10
  17.7 0.8 copy-start.11
  18.6 0.8 copy-start.12
  19.3 0.8 copy-start.13
  20.1 0.7 copy-start.14
  20.8 0.7 copy-start.15
  21.5 0.7 copy-start.16
  22.2 50.2 %copy-start.17 = (bf16[256,256]{1,0:T(8,128)(2,1)S(1)}, bf16[256,256]{1,0:T(8,128)(2,1)}, u32[]{:S(2)}) copy-start(bf16[256,256]{1,0:T(8,128)(2,1)} %param.26) | copy-start | bytes 393220
Sparse Core Ops, SparseCore 0:
  72.5 144.6 all-gather.2

commit v2 on v1

--- a/solution.py
+++ b/solution.py
@@ -277,22 +277,143 @@
     )(query, key_proj, value, filt, cotangent, skip, suffix_start, *[jnp.asarray(t) for t in tables])
 
 
+def project_kernel(
+    columns,
+    grads, own_weight, other_weight, layer_input,
+    input_grad, attribution,
+    gathered, partial, arrived, scores,
+    send_sem, recv_sem, part_sem, score_send_sem, score_recv_sem,
+):
+    tokens, features = layer_input.shape
+    depth = grads.shape[1]
+    me = lax.axis_index("ch")
+    column, side = me // 2, lax.rem(me, 2)
+    partner = 2 * column + (1 - side)
+    peers = 2 * columns
+
+    barrier = pltpu.get_barrier_semaphore()
+    for step in range(1, peers):
+        pl.semaphore_signal(barrier, inc=1, device_id={"ch": lax.rem(me + step, peers)}, device_id_type=MESH)
+    pl.semaphore_wait(barrier, peers - 1)
+
+    def gather(step):
+        return pltpu.make_async_remote_copy(
+            src_ref=grads,
+            dst_ref=gathered.at[step],
+            send_sem=send_sem.at[step],
+            recv_sem=recv_sem.at[step],
+            device_id={"ch": 2 * lax.rem(column + columns - step, columns) + side},
+            device_id_type=MESH,
+        )
+
+    for step in range(1, columns):
+        gather(step).start()
+
+    def block(weight, step):
+        place = lax.rem(column + step, columns) * depth
+        return weight[pl.ds(pl.multiple_of(place, depth), depth), :]
+
+    other = dot(grads[...], block(other_weight, 0))
+    own = dot(grads[...], block(own_weight, 0))
+    for step in range(1, columns):
+        gather(step).wait_recv()
+        other += dot(gathered[step], block(other_weight, step))
+        if step < columns - 1:
+            own += dot(gathered[step], block(own_weight, step))
+    partial[...] = other.astype(BF16)
+    exchange = pltpu.make_async_remote_copy(
+        src_ref=partial,
+        dst_ref=arrived,
+        send_sem=part_sem.at[0],
+        recv_sem=part_sem.at[1],
+        device_id={"ch": partner},
+        device_id_type=MESH,
+    )
+    exchange.start()
+    if columns > 1:
+        own += dot(gathered[columns - 1], block(own_weight, columns - 1))
+    exchange.wait()
+    full_grad = own + arrived[...].astype(F32)
+    input_grad[...] = full_grad.astype(BF16)
+    weighted = full_grad * layer_input[...].astype(F32)
+    folded = weighted[:, :LANES]
+    for start in range(LANES, features, LANES):
+        folded = folded + weighted[:, start : start + LANES]
+    score = jnp.sum(folded.T, axis=0, keepdims=True)
+    scores[me] = jnp.broadcast_to(score, (8, tokens))
+
+    def share(step, index):
+        return pltpu.make_async_remote_copy(
+            src_ref=scores.at[me],
+            dst_ref=scores.at[index],
+            send_sem=score_send_sem.at[step],
+            recv_sem=score_recv_sem.at[index],
+            device_id={"ch": lax.rem(me + step, peers)},
+            device_id_type=MESH,
+        )
+
+    for step in range(1, peers):
+        share(step, me).start()
+    for step in range(1, peers):
+        copy = share(step, lax.rem(me + step, peers))
+        copy.wait_recv()
+        copy.wait_send()
+    total = scores[0]
+    for index in range(1, peers):
+        total = total + scores[index]
+    attribution[...] = total[0:1, :]
+    for step in range(1, columns):
+        gather(step).wait_send()
+
+
+def project(grads, own_weight, other_weight, layer_input):
+    tokens, features = layer_input.shape
+    peers = lax.axis_size("ch")
+    columns = peers // 2
+    vmem = pl.BlockSpec(memory_space=pltpu.VMEM)
+    return pl.pallas_call(
+        functools.partial(project_kernel, columns),
+        out_shape=(jax.ShapeDtypeStruct((tokens, features), BF16), jax.ShapeDtypeStruct((1, tokens), F32)),
+        in_specs=[vmem] * 4,
+        out_specs=(vmem, vmem),
+        scratch_shapes=[
+            pltpu.VMEM((columns, tokens, grads.shape[1]), BF16),
+            pltpu.VMEM((tokens, features), BF16),
+            pltpu.VMEM((tokens, features), BF16),
+            pltpu.VMEM((peers, 8, tokens), F32),
+            pltpu.SemaphoreType.DMA((columns,)),
+            pltpu.SemaphoreType.DMA((columns,)),
+            pltpu.SemaphoreType.DMA((2,)),
+            pltpu.SemaphoreType.DMA((peers,)),
+            pltpu.SemaphoreType.DMA((peers,)),
+        ],
+        compiler_params=pltpu.CompilerParams(
+            collective_id=1, has_side_effects=True, vmem_limit_bytes=48 * 1024 * 1024
+        ),
+        name="project",
+    )(grads, own_weight, other_weight, layer_input)
+
+
+def sided_weights(in_weight, width):
+    peers = lax.axis_size("ch")
+    parts = lax.axis_size("seq")
+    features = in_weight.shape[1]
+    side = lax.axis_index("ch") % 2
+    rows = in_weight.reshape(3, peers // 2, 2, width, features).transpose(2, 1, 0, 3, 4).reshape(2, -1, features)
+    own = lax.dynamic_index_in_dim(rows, side, 0, keepdims=False)
+    theirs = lax.dynamic_index_in_dim(rows, 1 - side, 0, keepdims=False)
+    share = theirs.shape[0] // parts
+    mine = lax.dynamic_slice_in_dim(theirs, lax.axis_index("seq") * share, share, 0)
+    swapped = lax.ppermute(mine, "ch", [(i, i ^ 1) for i in range(peers)])
+    return own, lax.all_gather(swapped, "seq", axis=0, tiled=True)
+
+
 def shards(query, key_proj, value, filt, skip, cotangent, suffix_start, layer_input, in_weight):
     tokens, width = query.shape
+    own, other = sided_weights(in_weight, width)
     grads = projection_grads(query, key_proj, value, filt, cotangent, skip[None, :], suffix_start)
-    features = in_weight.shape[1]
-    weights = in_weight.reshape(3, in_weight.shape[0] // 3, features)
-    gathered = lax.all_gather(grads, "ch", axis=0)
-    gathered = gathered.reshape(-1, tokens, 3, width)
-    full_grad = jnp.einsum(
-        "atjc,jacd->td",
-        gathered,
-        weights.reshape(3, -1, width, features),
-        preferred_element_type=F32,
-    )
-    partial_score = jnp.sum(full_grad * layer_input.astype(F32), axis=1)
-    attribution = lax.psum(partial_score, "ch")
-    return full_grad.astype(BF16), attribution
+    input_grad, attribution = project(grads, own, other, layer_input)
+    return input_grad, attribution[0]
 
 
 def solution(mesh):

time: 286 us -> 220 us (0.77)
  the two profiles are of different devices: /device:TPU:160 before, /device:TPU:104 now
where the time goes in v2:
time: 220 us; the launch traced here: 219 us
  Pallas kernels  108 us (49%)
  waiting for transfers between devices  71.8 us (33%)
  between operations  14.9 us (7%)
  starting transfers between devices  13.1 us (6%)
  local copies, waits for them, and re-layouts  11.1 us (5%)
    all_gather x1, waiting for transfers between devices, sided_weights(): return (own, lax.all_gather(swapped, 'seq', axis=0, tiled=True))  70 us
    pallas_call x1, Pallas kernels, project(): pl.pallas_call(functools.partial(project_kernel, columns), out_shape=(jax...  56.7 us
    pallas_call x1, Pallas kernels, projection_grads(): pl.pallas_call(functools.partial(conv_kernel, chips), out_shape=jax.Shape...  51.7 us
    ppermute x1, starting transfers between devices, sided_weights(): swapped = lax.ppermute(mine, 'ch', [(i, i ^ 1) for i in range(peers)])  13 us
    unnamed x42, local copies, waits for them, and re-layouts  6.22 us
  transfers between devices with their start and end apart: 2, of which 2 were waited for; matrix products, arithmetic and copies ran while one was open for 0% of the time, Pallas kernels for 24%

profile of v2, /device:TPU:104, one launch (start us, length us, event | category | flops | bytes accessed | tf_op | source)
XLA Modules:
  0.0 219.2 jit_solution(2968726761705068965)
XLA Ops:
  7.2 0.0 all-gather.2.cloned.1.call-start
  7.2 0.0 copy-start.1
  7.2 0.0 copy-start.2
  7.2 0.0 copy-start.3
  7.3 0.0 copy-start.4
  7.3 0.0 copy-start.5
  7.3 0.0 copy-start.6
  7.3 0.0 copy-start.7
  7.3 0.0 copy-start.8
  7.3 0.0 copy-start.9
  7.3 0.0 copy-start.11
  7.3 0.0 copy-start.12
  7.3 0.0 copy-start.15
  7.4 4.0 %copy.21 = bf16[2,4,3,256,256]{4,3,2,1,0:T(8,128)(2,1)} copy(bf16[2,4,3,256,256]{4,3,0,1,2:T(8,128)(2,1)} %bitcast.14) | data formatting | bytes 6291456 | tf_op jit(solution)/shard_map/transpose | solution.py:402
  11.3 0.8 dynamic-slice_bitcast_fusion.1
  12.1 13.0 %collective-permute-start = (bf16[48,256]{1,0:T(8,128)(2,1)S(1)}, bf16[48,256]{1,0:T(8,128)(2,1)S(1)}, u32[]{:S(2)}, u32[]{:S(2)}) collective-permute-start(bf16[48,256]{1,0:T(8,128)(2,1)S(1)} %dynamic-slice_bitcast_fusion.1), channel_id=1, source_target_pairs={{0,1},{1,0},{2,3},{3,2},{4,5},{5,4},{6,7},{7,6},{8,9},{9,8},{10,11... | collective-permute-start | bytes 73736 | tf_op jit(solution)/shard_map/ppermute | solution.py:407
  25.1 1.8 collective-permute-done
  26.9 0.0 copy-start.19
  26.9 0.6 copy-done.19
  27.5 0.0 all-gather.2.cloned.1.call-update
  28.2 0.0 copy-done.1
  28.2 0.0 copy-done.2
  28.2 0.0 copy-done.3
  28.2 0.0 copy-done.4
  28.2 0.0 copy-done.5
  28.3 0.0 copy-done.6
  28.3 0.0 copy-done.7
  28.3 0.0 copy-done.8
  28.3 0.0 copy-done.9
  28.3 0.0 copy-done.11
  28.3 0.0 copy-done.12
  28.3 0.0 copy-done.15
  28.3 0.0 copy-start.13
  28.3 0.7 copy-done.13
  29.1 0.0 copy-start.14
  29.1 0.8 copy-done.14
  29.8 0.0 copy-start.16
  29.8 0.7 copy-done.16
  30.6 0.0 copy-start.17
  30.6 0.7 copy-done.17
  31.2 0.0 copy-start.18
  31.2 0.0 copy-start.10
  31.2 51.7 %conv_grads.1.grads = bf16[256,768]{1,0:T(8,128)(2,1)S(1)} custom-call(bf16[256,256]{1,0:T(8,128)(2,1)S(1)} %copy-done.6, bf16[256,256]{1,0:T(8,128)(2,1)S(1)} %copy-done.7, bf16[256,256]{1,0:T(8,128)(2,1)S(1)} %copy-done.8, f32[256,256]{1,0:T(8,128)S(1)} %copy-done.5, bf16[256,256]{1,0:T(8,128)(2,1)S(1)} %copy-done.9, f32[1,256]{1,0:T(1,128)S(1)} %bitcast.10, ...), custom_call_target="tpu_custom_call" | custom-call | tf_op jit(solution)/shard_map/conv_grads/pallas_call | solution.py:248
  82.9 0.0 copy-done.18
  82.9 0.1 dynamic-slice_bitcast_fusion.own_weight
  83.1 70.0 %all-gather.2.cloned.1.call-done.other_weight = bf16[3072,256]{1,0:T(8,128)(2,1)} async-done(((bf16[48,256]{1,0:T(8,128)(2,1)}), bf16[3072,256]{1,0:T(8,128)(2,1)}) %all-gather.2.cloned.1.call-update) | async-done | bytes 1572880 | tf_op jit(solution)/shard_map/all_gather | solution.py:408
  153.1 0.0 copy-done.10
  153.1 0.0 copy-start
  153.1 1.4 copy-done
  154.5 56.7 %project.1 = (bf16[256,256]{1,0:T(8,128)(2,1)S(1)}, f32[1,256]{1,0:T(1,128)S(1)}) custom-call(bf16[256,768]{1,0:T(8,128)(2,1)S(1)} %conv_grads.1.grads, bf16[3072,256]{1,0:T(8,128)(2,1)S(1)} %dynamic-slice_bitcast_fusion.own_weight, bf16[3072,256]{1,0:T(8,128)(2,1)S(1)} %copy-done, bf16[256,256]{1,0:T(8,128)(2,1)S(1)} %copy-done.10), custom_call_target="tpu_custom_call" | custom-call | tf_op jit(solution)/shard_map/project/pallas_call | solution.py:374
  211.1 0.7 copy.25
  211.8 0.6 copy.26
Async XLA Ops:
  7.2 145.9 %all-gather.2.cloned.1.call-start = ((), (), s32[]{:S(2)}) async-start(), calls=%async_computation | async-start | bytes 1597440 | tf_op jit(solution)/shard_map/all_gather | solution.py:408
  7.2 21.0 %copy-start.1 = (bf16[512,512]{1,0:T(8,128)(2,1)S(1)}, bf16[512,512]{1,0:T(8,128)(2,1)}, u32[]{:S(2)}) copy-start(bf16[512,512]{1,0:T(8,128)(2,1)} %constant.75.clone.two_hi) | copy-start | bytes 1572868
  7.2 21.0 %copy-start.2 = (bf16[512,512]{1,0:T(8,128)(2,1)S(1)}, bf16[512,512]{1,0:T(8,128)(2,1)}, u32[]{:S(2)}) copy-start(bf16[512,512]{1,0:T(8,128)(2,1)} %constant.76.clone.two_lo) | copy-start | bytes 1572868
  7.2 21.0 %copy-start.3 = (bf16[512,512]{1,0:T(8,128)(2,1)S(1)}, bf16[512,512]{1,0:T(8,128)(2,1)}, u32[]{:S(2)}) copy-start(bf16[512,512]{1,0:T(8,128)(2,1)} %constant.77.clone.inv_hi) | copy-start | bytes 1572868
  7.3 21.0 %copy-start.4 = (bf16[512,512]{1,0:T(8,128)(2,1)S(1)}, bf16[512,512]{1,0:T(8,128)(2,1)}, u32[]{:S(2)}) copy-start(bf16[512,512]{1,0:T(8,128)(2,1)} %constant.78.clone.inv_lo) | copy-start | bytes 1572868
  7.3 21.0 %copy-start.5 = (f32[256,256]{1,0:T(8,128)S(1)}, f32[256,256]{1,0:T(8,128)}, u32[]{:S(2)}) copy-start(f32[256,256]{1,0:T(8,128)} %filt.1) | copy-start | bytes 786436
  7.3 21.0 %copy-start.6 = (bf16[256,256]{1,0:T(8,128)(2,1)S(1)}, bf16[256,256]{1,0:T(8,128)(2,1)}, u32[]{:S(2)}) copy-start(bf16[256,256]{1,0:T(8,128)(2,1)} %query.1) | copy-start | bytes 393220
  7.3 21.0 %copy-start.7 = (bf16[256,256]{1,0:T(8,128)(2,1)S(1)}, bf16[256,256]{1,0:T(8,128)(2,1)}, u32[]{:S(2)}) copy-start(bf16[256,256]{1,0:T(8,128)(2,1)} %key_proj.1) | copy-start | bytes 393220
  7.3 21.0 %copy-start.8 = (bf16[256,256]{1,0:T(8,128)(2,1)S(1)}, bf16[256,256]{1,0:T(8,128)(2,1)}, u32[]{:S(2)}) copy-start(bf16[256,256]{1,0:T(8,128)(2,1)} %value.1) | copy-start | bytes 393220
  7.3 21.0 %copy-start.9 = (bf16[256,256]{1,0:T(8,128)(2,1)S(1)}, bf16[256,256]{1,0:T(8,128)(2,1)}, u32[]{:S(2)}) copy-start(bf16[256,256]{1,0:T(8,128)(2,1)} %cotangent.1) | copy-start | bytes 393220
  7.3 21.0 %copy-start.11 = (f32[64,256]{1,0:T(8,128)S(1)}, f32[64,256]{1,0:T(8,128)}, u32[]{:S(2)}) copy-start(f32[64,256]{1,0:T(8,128)} %constant.81.clone.turn_cos) | copy-start | bytes 196612
  7.3 21.0 %copy-start.12 = (f32[64,256]{1,0:T(8,128)S(1)}, f32[64,256]{1,0:T(8,128)}, u32[]{:S(2)}) copy-start(f32[64,256]{1,0:T(8,128)} %constant.82.clone.turn_sin) | copy-start | bytes 196612
  7.3 21.0 %copy-start.15 = (bf16[64,128]{1,0:T(8,128)(2,1)S(1)}, bf16[64,128]{1,0:T(8,128)(2,1)}, u32[]{:S(2)}) copy-start(bf16[64,128]{1,0:T(8,128)(2,1)} %constant.79.clone.back_hi) | copy-start | bytes 49156
  12.1 14.8 %collective-permute-start = (bf16[48,256]{1,0:T(8,128)(2,1)S(1)}, bf16[48,256]{1,0:T(8,128)(2,1)S(1)}, u32[]{:S(2)}, u32[]{:S(2)}) collective-permute-start(bf16[48,256]{1,0:T(8,128)(2,1)S(1)} %dynamic-slice_bitcast_fusion.1), channel_id=1, source_target_pairs={{0,1},{1,0},{2,3},{3,2},{4,5},{5,4},{6,7},{7,6},{8,9},{9,8},{10,11... | collective-permute-start | bytes 73736 | tf_op jit(solution)/shard_map/ppermute | solution.py:407
  26.9 0.6 copy-start.19
  28.3 0.8 copy-start.13
  29.1 0.8 copy-start.14
  29.8 0.7 copy-start.16
  30.6 0.7 copy-start.17
  31.2 51.7 %copy-start.18 = (bf16[2,4,3,256,256]{4,3,2,1,0:T(8,128)(2,1)S(1)}, bf16[2,4,3,256,256]{4,3,2,1,0:T(8,128)(2,1)}, u32[]{:S(2)}) copy-start(bf16[2,4,3,256,256]{4,3,2,1,0:T(8,128)(2,1)} %copy.21) | copy-start | bytes 9437188
  31.2 121.8 %copy-start.10 = (bf16[256,256]{1,0:T(8,128)(2,1)S(1)}, bf16[256,256]{1,0:T(8,128)(2,1)}, u32[]{:S(2)}) copy-start(bf16[256,256]{1,0:T(8,128)(2,1)} %layer_input.1) | copy-start | bytes 393220
  153.1 1.4 copy-start
Sparse Core Ops, SparseCore 0:
  27.7 125.3 all-gather.1

commit v3 on v1

v3 whole, which is shorter than its diff:
```python
import functools

import jax
import jax.numpy as jnp
import numpy as np
from jax import lax
from jax.experimental import pallas as pl
from jax.experimental.pallas import tpu as pltpu
from jax.sharding import PartitionSpec as P

BF16 = jnp.bfloat16
F32 = jnp.float32
MESH = pl.DeviceIdType.MESH
LANES = 128
GROUP = 8
LINE = 8


def split_high_low(table):
    high = table.astype(np.float32).astype(BF16)
    low = (table - high.astype(np.float64)).astype(np.float32).astype(BF16)
    return high, low


def transform_tables(sources, tokens):
    chips = sources // 2
    order = np.arange(sources)
    place = 2 * (order % chips) + order // chips
    odd = np.arange(sources) + 0.5
    angle_one = 2.0 * np.pi / (2 * sources) * (odd[:, None] * place[None, :])
    first = np.concatenate([np.cos(angle_one), -np.sin(angle_one)], axis=0)
    length = 2 * sources * tokens
    turn = 2.0 * np.pi / length * (odd[:, None] * np.arange(tokens)[None, :])
    angle_two = 2.0 * np.pi / tokens * (np.arange(tokens)[:, None] * np.arange(tokens)[None, :] % tokens)
    cos_two, sin_two = np.cos(angle_two), np.sin(angle_two)
    second = np.block([[cos_two, -sin_two], [sin_two, cos_two]])
    back = first.T * (2.0 / length)
    tables = [np.concatenate(split_high_low(first), axis=1)]
    tables += split_high_low(second)
    tables += split_high_low(second.T)
    tables += split_high_low(back)
    tables += [np.cos(turn).astype(np.float32), np.sin(turn).astype(np.float32)]
    return tables


def halves(array):
    high = array.astype(BF16)
    return high, (array - high.astype(F32)).astype(BF16)


def dot(left, right):
    return jnp.dot(left, right, preferred_element_type=F32)


def to_blocks(signal, chips):
    turned = signal.T
    left = turned[:, :LANES].reshape(chips, GROUP, LANES)
    right = turned[:, LANES:].reshape(chips, GROUP, LANES)
    return jnp.concatenate([left, right], axis=1).astype(BF16)


def far_first(count):
    middle = count // 2
    return sorted(range(count), key=lambda step: (abs(step - middle), step))


def kernel(
    chips, columns,
    query_hbm, key_hbm, value_hbm, filt_hbm, cotangent_hbm, input_hbm, weight_hbm,
    one_hbm, two_hi_hbm, two_lo_hbm, inv_hi_hbm, inv_lo_hbm, back_hi_hbm, back_lo_hbm, cos_hbm, sin_hbm,
    skip, suffix_start,
    input_grad, attribution,
    query, key_proj, value, filt, cotangent, layer_input, own_weight, other_weight,
    one, two_hi, two_lo, inv_hi, inv_lo, back_hi, back_lo, turn_cos, turn_sin,
    send, recv, rows_f32, flat, spec_hi, spec_lo, spec, time_hi, time_lo, results, swapped, outgoing, returned,
    grads, gathered, partial, arrived, totals, scores,
    load_sem, send_sem, recv_sem, pair_sem, send_back_sem, recv_back_sem, pair_back_sem,
    share_sem, line_send_sem, line_recv_sem, ring_send_sem, ring_recv_sem, core_sem,
    gather_send_sem, gather_recv_sem, part_send_sem, part_recv_sem, score_send_sem, score_recv_sem,
):
    sources = 2 * chips
    line = min(LINE, chips)
    rings = chips // line
    peers = 2 * columns
    tokens, width = query.shape
    me, lane = lax.axis_index("seq"), lax.axis_index("ch")
    chip, core = me // 2, lax.rem(me, 2)
    y, z = chip // line, lax.rem(chip, line)
    column, side = lane // 2, lax.rem(lane, 2)

    def seat(dy, dz):
        return lax.rem(y + dy + rings, rings) * line + lax.rem(z + dz + line, line)

    def same_core(dy, dz):
        return {"seq": 2 * seat(dy, dz) + core}

    other_core = {"seq": 2 * chip + (1 - core)}
    other_side = {"ch": 2 * column + (1 - side)}

    def along_x(step):
        return {"ch": 2 * lax.rem(column + step + columns, columns) + side}

    def along_ch(step):
        return {"ch": lax.rem(lane + step + peers, peers)}

    barrier = pltpu.get_barrier_semaphore()

    def over_chips(body):
        for dz in far_first(line):
            def one_step(dy, carry, dz=dz):
                body(dy, dz)
                return carry

            lax.fori_loop(1 if dz == 0 else 0, rings, one_step, 0)

    def greet(device):
        pl.semaphore_signal(barrier, inc=1, device_id=device, device_id_type=MESH)

    over_chips(lambda dy, dz: greet(same_core(dy, dz)))
    greet(other_core)
    for step in range(1, peers):
        greet(along_ch(step))

    loads = [
        (key_hbm, key_proj), (value_hbm, value), (filt_hbm, filt), (cotangent_hbm, cotangent), (query_hbm, query),
        (one_hbm, one), (cos_hbm, turn_cos), (sin_hbm, turn_sin), (two_hi_hbm, two_hi), (two_lo_hbm, two_lo),
        (inv_hi_hbm, inv_hi), (inv_lo_hbm, inv_lo), (back_hi_hbm, back_hi), (back_lo_hbm, back_lo),
        (input_hbm, layer_input),
    ]
    loads += [(weight_hbm.at[:, 2 * index + side], own_weight.at[index]) for index in range(columns)]
    loads = [pltpu.make_async_copy(a, b, load_sem.at[i]) for i, (a, b) in enumerate(loads)]
    for load in loads:
        load.start()

    loads[0].wait()
    loads[1].wait()
    send[:, 0:16, :] = to_blocks(key_proj[...].astype(F32) * value[...].astype(F32), chips)
    loads[2].wait()
    send[:, 16:32, :] = to_blocks(filt[...], chips)
    loads[3].wait()
    loads[4].wait()
    positions = me * tokens + lax.broadcasted_iota(jnp.int32, (tokens, width), 0)
    grad_out = jnp.where(positions >= suffix_start[0], cotangent[...].astype(F32), 0.0)
    send[:, 32:48, :] = to_blocks(grad_out * query[...].astype(F32), chips)

    pl.semaphore_wait(barrier, chips + peers - 1)

    def forward(dy, dz, index):
        return pltpu.make_async_remote_copy(
            src_ref=send.at[seat(dy, dz)],
            dst_ref=recv.at[core, index],
            send_sem=send_sem.at[dy * line + dz],
            recv_sem=recv_sem.at[dy * line + dz],
            device_id=same_core(dy, dz),
            device_id_type=MESH,
        )

    over_chips(lambda dy, dz: forward(dy, dz, chip).start())

    per_column = sources // columns
    share_rows = width // per_column
    share = core * chips + chip
    share_column = share // per_column

    def rows_at(index, count):
        return pl.ds(pl.multiple_of(lax.rem(index, per_column) * share_rows, share_rows), count * share_rows)

    give_share = pltpu.make_async_remote_copy(
        src_ref=weight_hbm.at[:, 2 * share_column + (1 - side), rows_at(share, 1)],
        dst_ref=other_weight.at[share_column, :, rows_at(share, 1)],
        send_sem=share_sem.at[0],
        recv_sem=share_sem.at[1],
        device_id=other_side,
        device_id_type=MESH,
    )
    give_share.start()
    recv[core, chip] = send[chip]
    over_chips(lambda dy, dz: forward(dy, dz, seat(-dy, -dz)).wait_recv())

    theirs = pl.ds(pl.multiple_of(16 * (1 - core), 16), 32)
    swap = pltpu.make_async_remote_copy(
        src_ref=recv.at[core, :, theirs],
        dst_ref=recv.at[core, :, theirs],
        send_sem=pair_sem.at[0],
        recv_sem=pair_sem.at[1],
        device_id=other_core,
        device_id_type=MESH,
    )
    swap.start()

    def along_line(step, index):
        place = other_weight.at[share_column, :, rows_at(core * chips + y * line + index, 1)]
        return pltpu.make_async_remote_copy(
            src_ref=place,
            dst_ref=place,
            send_sem=line_send_sem.at[step],
            recv_sem=line_recv_sem.at[step],
            device_id=same_core(0, step),
            device_id_type=MESH,
        )

    give_share.wait_recv()
    for step in range(1, line):
        along_line(step, z).start()
    swap.wait_recv()

    for index in range(5, 14):
        loads[index].wait()
    sign = jnp.where(core == 0, 1.0, -1.0).astype(F32)
    for signal in range(2):
        if signal == 0:
            rows = recv[:, :, 16:32, :]
        else:
            rows = recv[:, :, pl.ds(pl.multiple_of(32 * core, 16), 16), :]
        rows_f32[...] = rows.astype(F32).reshape(sources * 16, LANES)
        for r in range(16):
            block = rows_f32[pl.ds(r, sources, stride=16), :].astype(BF16)
            flat[:sources, r * LANES : (r + 1) * LANES] = block
            flat[sources:, r * LANES : (r + 1) * LANES] = block
        stage = dot(one[...], flat[...])
        for r in range(16):
            half, channel = r // GROUP, r % GROUP
            span = slice(half * LANES, (half + 1) * LANES)
            real = stage[:sources, r * LANES : (r + 1) * LANES]
            imag = stage[sources:, r * LANES : (r + 1) * LANES]
            cos, sin = turn_cos[:, span], turn_sin[:, span]
            place = slice((signal * GROUP + channel) * sources, (signal * GROUP + channel + 1) * sources)
            spec_hi[place, span], spec_lo[place, span] = halves(real * cos + imag * sin)
            span = slice(tokens + half * LANES, tokens + (half + 1) * LANES)
            spec_hi[place, span], spec_lo[place, span] = halves(imag * cos - real * sin)
    spec[...] = (
        dot(spec_hi[...], two_hi[...]) + dot(spec_lo[...], two_hi[...]) + dot(spec_hi[...], two_lo[...])
    )
    count = GROUP * sources
    fr, fi = spec[:count, :tokens], spec[:count, tokens:] * sign
    pr, pi = spec[count:, :tokens], spec[count:, tokens:]
    product = jnp.concatenate([fr * pr - fi * pi, fr * pi + fi * pr], axis=1)
    prod_hi, prod_lo = halves(product)
    inverse = dot(prod_hi, inv_hi[...]) + dot(prod_lo, inv_hi[...]) + dot(prod_hi, inv_lo[...])
    for r in range(16):
        half, channel = r // GROUP, r % GROUP
        span = slice(half * LANES, (half + 1) * LANES)
        place = slice(channel * sources, (channel + 1) * sources)
        real = inverse[place, span]
        imag = inverse[place, tokens + half * LANES : tokens + (half + 1) * LANES]
        cos, sin = turn_cos[:, span], turn_sin[:, span]
        span = slice(r * LANES, (r + 1) * LANES)
        time_hi[:sources, span], time_lo[:sources, span] = halves(real * cos - imag * sin)
        time_hi[sources:, span], time_lo[sources:, span] = halves(imag * cos + real * sin)
    result = dot(back_hi[...], time_hi[...]) + dot(back_lo[...], time_hi[...]) + dot(back_hi[...], time_lo[...])
    for r in range(16):
        rows_f32[pl.ds(r, sources, stride=16), :] = result[:, r * LANES : (r + 1) * LANES]
    results[...] = rows_f32[...].reshape(2, chips, 16, LANES).astype(BF16)

    swap_back = pltpu.make_async_remote_copy(
        src_ref=results.at[1 - core],
        dst_ref=swapped,
        send_sem=pair_back_sem.at[0],
        recv_sem=pair_back_sem.at[1],
        device_id=other_core,
        device_id_type=MESH,
    )
    swap_back.start()

    def along_ring(step, index):
        first = core * chips + index * line
        place = other_weight.at[first // per_column, :, rows_at(first, line)]
        return pltpu.make_async_remote_copy(
            src_ref=place,
            dst_ref=place,
            send_sem=ring_send_sem.at[step],
            recv_sem=ring_recv_sem.at[step],
            device_id=same_core(step, 0),
            device_id_type=MESH,
        )

    mine = results[core].astype(F32)
    swap_back.wait_recv()
    given = swapped[...].astype(F32)
    conv = jnp.where(core == 0, mine, given)
    corr = jnp.where(core == 0, given, mine)
    for half in range(2):
        span = slice(half * GROUP, (half + 1) * GROUP)
        outgoing[half] = jnp.concatenate([conv[:, span], corr[:, span]], axis=1).astype(BF16)

    def backward(half, dy, dz, index):
        return pltpu.make_async_remote_copy(
            src_ref=outgoing.at[half, seat(dy, dz)],
            dst_ref=returned.at[half, index],
            send_sem=send_back_sem.at[half, dy * line + dz],
            recv_sem=recv_back_sem.at[half, dy * line + dz],
            device_id=same_core(dy, dz),
            device_id_type=MESH,
        )

    for half in range(2):
        over_chips(lambda dy, dz: backward(half, dy, dz, chip).start())
        returned[half, chip] = outgoing[half, chip]
    for step in range(1, line):
        along_line(step, lax.rem(z - step + line, line)).wait_recv()
    for step in range(1, rings):
        along_ring(step, y).start()

    def gather(half, step):
        return pltpu.make_async_remote_copy(
            src_ref=grads.at[half],
            dst_ref=gathered.at[half, step],
            send_sem=gather_send_sem.at[half, step],
            recv_sem=gather_recv_sem.at[half, step],
            device_id=along_x(-step),
            device_id_type=MESH,
        )

    gains = skip[...]
    for half in range(2):
        over_chips(lambda dy, dz: backward(half, dy, dz, seat(-dy, -dz)).wait_recv())
        span = slice(half * LANES, (half + 1) * LANES)
        blocks = returned[half].astype(F32)
        conv_out = blocks[:, :GROUP].reshape(width, LANES).T
        corr_out = blocks[:, GROUP:].reshape(width, LANES).T
        keys = key_proj[span, :].astype(F32)
        values = value[span, :].astype(F32)
        positions = me * tokens + half * LANES + lax.broadcasted_iota(jnp.int32, (LANES, width), 0)
        grad_out = jnp.where(positions >= suffix_start[0], cotangent[span, :].astype(F32), 0.0)
        grad_mixed = corr_out + gains * (grad_out * query[span, :].astype(F32))
        grads[half, :, :width] = (grad_out * (conv_out + gains * (keys * values))).astype(BF16)
        grads[half, :, width : 2 * width] = (grad_mixed * values).astype(BF16)
        grads[half, :, 2 * width :] = (grad_mixed * keys).astype(BF16)
        for step in range(1, columns):
            gather(half, step).start()

    for step in range(1, rings):
        along_ring(step, lax.rem(y - step + rings, rings)).wait_recv()
    portion = other_weight.at[pl.ds(core * (columns // 2), columns // 2)]
    give_core = pltpu.make_async_remote_copy(
        src_ref=portion,
        dst_ref=portion,
        send_sem=core_sem.at[0],
        recv_sem=core_sem.at[1],
        device_id=other_core,
        device_id_type=MESH,
    )
    give_core.start()
    for index in range(14, len(loads)):
        loads[index].wait()
    give_core.wait_recv()

    def exchange(half):
        return pltpu.make_async_remote_copy(
            src_ref=partial.at[half],
            dst_ref=arrived.at[half],
            send_sem=part_send_sem.at[half],
            recv_sem=part_recv_sem.at[half],
            device_id=other_side,
            device_id_type=MESH,
        )

    def product_of(half, step, weight):
        left = grads[half] if step == 0 else gathered[half, step]
        return dot(left, weight[lax.rem(column + step, columns)].reshape(3 * width, -1))

    for half in range(2):
        other = product_of(half, 0, other_weight)
        own = product_of(half, 0, own_weight)
        for step in range(1, columns):
            gather(half, step).wait_recv()
            other += product_of(half, step, other_weight)
        partial[half] = other.astype(BF16)
        exchange(half).start()
        for step in range(1, columns):
            own += product_of(half, step, own_weight)
        totals[half] = own

    parts = []
    for half in range(2):
        span = slice(half * LANES, (half + 1) * LANES)
        exchange(half).wait_recv()
        full_grad = totals[half] + arrived[half].astype(F32)
        input_grad[span, :] = full_grad.astype(BF16)
        weighted = full_grad * layer_input[span, :].astype(F32)
        features = weighted.shape[1]
        folded = weighted[:, : min(LANES, features)]
        for start in range(LANES, features, LANES):
            folded = folded + weighted[:, start : start + LANES]
        parts.append(jnp.sum(folded.T, axis=0, keepdims=True))
    scores[lane] = jnp.broadcast_to(jnp.concatenate(parts, axis=1), (8, tokens))

    def tell(step, index):
        return pltpu.make_async_remote_copy(
            src_ref=scores.at[index],
            dst_ref=scores.at[index],
            send_sem=score_send_sem.at[step],
            recv_sem=score_recv_sem.at[step],
            device_id=along_ch(step),
            device_id_type=MESH,
        )

    for step in range(1, peers):
        tell(step, lane).start()

    over_chips(lambda dy, dz: forward(dy, dz, chip).wait_send())
    give_share.wait_send()
    swap.wait_send()
    swap_back.wait_send()
    give_core.wait_send()
    for step in range(1, line):
        along_line(step, z).wait_send()
    for step in range(1, rings):
        along_ring(step, y).wait_send()
    for half in range(2):
        over_chips(lambda dy, dz: backward(half, dy, dz, chip).wait_send())
        for step in range(1, columns):
            gather(half, step).wait_send()
        exchange(half).wait_send()

    for step in range(1, peers):
        tell(step, lax.rem(lane - step + peers, peers)).wait_recv()
    total = scores[0]
    for index in range(1, peers):
        total = total + scores[index]
    attribution[...] = total[0:1, :]
    for step in range(1, peers):
        tell(step, lane).wait_send()


def shards(query, key_proj, value, filt, skip, cotangent, suffix_start, layer_input, in_weight):
    tokens, width = query.shape
    features = in_weight.shape[1]
    sources, peers = lax.axis_size("seq"), lax.axis_size("ch")
    chips, columns = sources // 2, peers // 2
    line = min(LINE, chips)
    rings = chips // line
    tables = transform_tables(sources, tokens)
    count = GROUP * sources
    vmem = pl.BlockSpec(memory_space=pltpu.VMEM)
    smem = pl.BlockSpec(memory_space=pltpu.SMEM)
    hbm = pl.BlockSpec(memory_space=pl.ANY)
    dma = pltpu.SemaphoreType.DMA
    block = pltpu.VMEM((tokens, width), BF16)
    weight_block = pltpu.VMEM((columns, 3, width, features), BF16)
    input_grad, attribution = pl.pallas_call(
        functools.partial(kernel, chips, columns),
        out_shape=(jax.ShapeDtypeStruct((tokens, features), BF16), jax.ShapeDtypeStruct((1, tokens), F32)),
        in_specs=[hbm] * (7 + len(tables)) + [vmem, smem],
        out_specs=(vmem, vmem),
        scratch_shapes=[
            block, block, block, pltpu.VMEM((tokens, width), F32), block, pltpu.VMEM((tokens, features), BF16),
            weight_block, weight_block,
            *[pltpu.VMEM(table.shape, table.dtype) for table in tables],
            pltpu.VMEM((chips, 48, LANES), BF16),
            pltpu.VMEM((2, chips, 48, LANES), BF16),
            pltpu.VMEM((sources * 16, LANES), F32),
            pltpu.VMEM((2 * sources, 16 * LANES), BF16),
            pltpu.VMEM((2 * count, 2 * tokens), BF16),
            pltpu.VMEM((2 * count, 2 * tokens), BF16),
            pltpu.VMEM((2 * count, 2 * tokens), F32),
            pltpu.VMEM((2 * sources, 16 * LANES), BF16),
            pltpu.VMEM((2 * sources, 16 * LANES), BF16),
            pltpu.VMEM((2, chips, 16, LANES), BF16),
            pltpu.VMEM((chips, 16, LANES), BF16),
            pltpu.VMEM((2, chips, 16, LANES), BF16),
            pltpu.VMEM((2, chips, 16, LANES), BF16),
            pltpu.VMEM((2, LANES, 3 * width), BF16),
            pltpu.VMEM((2, columns, LANES, 3 * width), BF16),
            pltpu.VMEM((2, LANES, features), BF16),
            pltpu.VMEM((2, LANES, features), BF16),
            pltpu.VMEM((2, LANES, features), F32),
            pltpu.VMEM((peers, 8, tokens), F32),
            dma((15 + columns,)),
            dma((chips,)), dma((chips,)), dma((2,)),
            dma((2, chips)), dma((2, chips)), dma((2,)),
            dma((2,)), dma((line,)), dma((line,)), dma((rings,)), dma((rings,)), dma((2,)),
            dma((2, columns)), dma((2, columns)), dma((2,)), dma((2,)), dma((peers,)), dma((peers,)),
        ],
        compiler_params=pltpu.CompilerParams(
            collective_id=0, has_side_effects=True, vmem_limit_bytes=56 * 1024 * 1024
        ),
        name="conv_backward",
    )(
        query, key_proj, value, filt, cotangent, layer_input, in_weight.reshape(3, peers, width, features),
        *[jnp.asarray(table) for table in tables],
        skip[None, :], suffix_start,
    )
    return input_grad, attribution[0]


def solution(mesh):
    in_specs = (
        P("seq", "ch"),
        P("seq", "ch"),
        P("seq", "ch"),
        P("seq", "ch"),
        P("ch"),
        P("seq", "ch"),
        P(),
        P("seq", "ch"),
        P(None, "ch"),
    )
    out_specs = (P("seq", "ch"), P("seq"))
    return jax.shard_map(shards, mesh=mesh, in_specs=in_specs, out_specs=out_specs, check_vma=False)
```

time: 286 us -> 106 us (0.37)
  the two profiles are of different devices: /device:TPU:160 before, /device:TPU:32 now
where the time goes in v3:
time: 106 us
  Pallas kernels  102 us (96%)
  local copies, waits for them, and re-layouts  2.8 us (3%)
  between operations  1.29 us (1%)
    pallas_call x1, Pallas kernels, shards(): pl.pallas_call(functools.partial(kernel, chips, columns), out_shape=(jax....  102 us
    unnamed x2, local copies, waits for them, and re-layouts  2.8 us

profile of v3, /device:TPU:32, one launch (start us, length us, event | category | flops | bytes accessed | tf_op | source)
XLA Modules:
  0.0 105.8 jit_solution(13077146831149640342)
XLA Ops:
  1.3 101.7 %conv_backward.1 = (bf16[256,256]{1,0:T(8,128)(2,1)}, f32[1,256]{1,0:T(1,128)}) custom-call(bf16[256,256]{1,0:T(8,128)(2,1)} %query_hbm.1, bf16[256,256]{1,0:T(8,128)(2,1)} %key_hbm.1, bf16[256,256]{1,0:T(8,128)(2,1)} %value_hbm.1, f32[256,256]{1,0:T(8,128)} %filt_hbm.1, bf16[256,256]{1,0:T(8,128)(2,1)} %cotangent_hbm.1, bf16[256,256]{1,0:T(8,128)(2,1)} %input_hbm.1, ...), custom_call_target="tpu_custom_call" | custom-call | tf_op jit(solution)/shard_map/conv_backward/pallas_call | solution.py:441
  103.0 1.6 %copy.23 = bf16[256,256]{1,0:T(8,128)(2,1)} copy(bf16[256,256]{1,0:T(8,128)(2,1)} %get-tuple-element.8) | data formatting | bytes 262144
  104.6 1.2 %copy.24 = f32[256]{0:T(256)} copy(f32[256]{0:T(256)} %bitcast.4) | data formatting | bytes 2048

commit v4 on v3

--- a/solution.py
+++ b/solution.py
@@ -14,6 +14,7 @@
 LANES = 128
 GROUP = 8
 LINE = 8
+PART = 64
 
 
 def split_high_low(table):
@@ -70,13 +71,14 @@
     one_hbm, two_hi_hbm, two_lo_hbm, inv_hi_hbm, inv_lo_hbm, back_hi_hbm, back_lo_hbm, cos_hbm, sin_hbm,
     skip, suffix_start,
     input_grad, attribution,
-    query, key_proj, value, filt, cotangent, layer_input, own_weight, other_weight,
+    query, key_proj, value, filt, cotangent, layer_input, other_input, own_weight, other_weight,
     one, two_hi, two_lo, inv_hi, inv_lo, back_hi, back_lo, turn_cos, turn_sin,
     send, recv, rows_f32, flat, spec_hi, spec_lo, spec, time_hi, time_lo, results, swapped, outgoing, returned,
-    grads, gathered, partial, arrived, totals, scores,
+    grads, gathered, partial, arrived, totals, others, scores,
     load_sem, send_sem, recv_sem, pair_sem, send_back_sem, recv_back_sem, pair_back_sem,
     share_sem, line_send_sem, line_recv_sem, ring_send_sem, ring_recv_sem, core_sem,
-    gather_send_sem, gather_recv_sem, part_send_sem, part_recv_sem, score_send_sem, score_recv_sem,
+    input_sem,
+    gather_send_sem, gather_recv_sem, hand_send_sem, hand_recv_sem, part_send_sem, part_recv_sem, score_send_sem, score_recv_sem,
 ):
     sources = 2 * chips
     line = min(LINE, chips)
@@ -116,11 +118,10 @@
     def greet(device):
         pl.semaphore_signal(barrier, inc=1, device_id=device, device_id_type=MESH)
 
+    for step in range(1, peers):
+        greet(along_ch(step))
     over_chips(lambda dy, dz: greet(same_core(dy, dz)))
     greet(other_core)
-    for step in range(1, peers):
-        greet(along_ch(step))
-
     loads = [
         (key_hbm, key_proj), (value_hbm, value), (filt_hbm, filt), (cotangent_hbm, cotangent), (query_hbm, query),
         (one_hbm, one), (cos_hbm, turn_cos), (sin_hbm, turn_sin), (two_hi_hbm, two_hi), (two_lo_hbm, two_lo),
@@ -155,8 +156,6 @@
             device_id_type=MESH,
         )
 
-    over_chips(lambda dy, dz: forward(dy, dz, chip).start())
-
     per_column = sources // columns
     share_rows = width // per_column
     share = core * chips + chip
@@ -174,7 +173,36 @@
         device_id_type=MESH,
     )
     give_share.start()
+    over_chips(lambda dy, dz: forward(dy, dz, chip).start())
     recv[core, chip] = send[chip]
+
+    def mirror(index, distance):
+        return index + distance * (1 - 2 * lax.rem(index // distance, 2))
+
+    def along_line(step, block, owner):
+        place = other_weight.at[share_column, :, rows_at(core * chips + y * line + (mirror(owner) if block else owner), 1)]
+        target = mirror(z) if step == 0 else ahead(step)
+        return pltpu.make_async_remote_copy(
+            src_ref=place,
+            dst_ref=place,
+            send_sem=line_send_sem.at[2 * step + block],
+            recv_sem=line_recv_sem.at[2 * step + block],
+            device_id=same_core(0, target - z),
+            device_id_type=MESH,
+        )
+
+    half_line = line // 2
+    within = [(step, block) for step in range(1, half_line) for block in range(2)]
+
+    def mirror(index):
+        return index + half_line * (1 - 2 * (index // half_line))
+
+    def ahead(step):
+        return z // half_line * half_line + lax.rem(z + step + half_line, half_line)
+
+    give_share.wait_recv()
+    if half_line:
+        along_line(0, 0, z).start()
     over_chips(lambda dy, dz: forward(dy, dz, seat(-dy, -dz)).wait_recv())
 
     theirs = pl.ds(pl.multiple_of(16 * (1 - core), 16), 32)
@@ -188,21 +216,22 @@
     )
     swap.start()
 
-    def along_line(step, index):
-        place = other_weight.at[share_column, :, rows_at(core * chips + y * line + index, 1)]
-        return pltpu.make_async_remote_copy(
-            src_ref=place,
-            dst_ref=place,
-            send_sem=line_send_sem.at[step],
-            recv_sem=line_recv_sem.at[step],
-            device_id=same_core(0, step),
-            device_id_type=MESH,
-        )
-
-    give_share.wait_recv()
-    for step in range(1, line):
-        along_line(step, z).start()
     swap.wait_recv()
+    if half_line:
+        along_line(0, 0, mirror(z)).wait_recv()
+    for step, block in within:
+        along_line(step, block, z).start()
+
+    def lend_input():
+        place = pl.ds(LANES, LANES)
+        return pltpu.make_async_remote_copy(
+            src_ref=input_hbm.at[place],
+            dst_ref=other_input,
+            send_sem=input_sem.at[0],
+            recv_sem=input_sem.at[1],
+            device_id=other_side,
+            device_id_type=MESH,
+        )
 
     for index in range(5, 14):
         loads[index].wait()
@@ -274,6 +303,10 @@
             device_id_type=MESH,
         )
 
+    for step, block in within:
+        along_line(step, block, ahead(-step)).wait_recv()
+    for step in range(1, rings):
+        along_ring(step, y).start()
     mine = results[core].astype(F32)
     swap_back.wait_recv()
     given = swapped[...].astype(F32)
@@ -296,24 +329,46 @@
     for half in range(2):
         over_chips(lambda dy, dz: backward(half, dy, dz, chip).start())
         returned[half, chip] = outgoing[half, chip]
-    for step in range(1, line):
-        along_line(step, lax.rem(z - step + line, line)).wait_recv()
-    for step in range(1, rings):
-        along_ring(step, y).start()
-
-    def gather(half, step):
-        return pltpu.make_async_remote_copy(
-            src_ref=grads.at[half],
-            dst_ref=gathered.at[half, step],
-            send_sem=gather_send_sem.at[half, step],
-            recv_sem=gather_recv_sem.at[half, step],
+
+    def gather(part, step):
+        return pltpu.make_async_remote_copy(
+            src_ref=grads.at[part],
+            dst_ref=gathered.at[part, step],
+            send_sem=gather_send_sem.at[part, step],
+            recv_sem=gather_recv_sem.at[part, step],
             device_id=along_x(-step),
             device_id_type=MESH,
         )
 
+    relayed = columns == 4
+    near = (1, 3) if relayed else tuple(range(1, columns))
+
+    def hand_on(part, source):
+        span = pl.ds(PART // 2, PART // 2) if source == 1 else pl.ds(0, PART // 2)
+        return pltpu.make_async_remote_copy(
+            src_ref=gathered.at[part, source, span],
+            dst_ref=gathered.at[part, 2, span],
+            send_sem=hand_send_sem.at[part, source // 2],
+            recv_sem=hand_recv_sem.at[part, source // 2],
+            device_id=along_x(-source),
+            device_id_type=MESH,
+        )
+
+    def end_near(half):
+        for part in parts_of(half):
+            for step in near:
+                gather(part, step).wait_recv()
+                if relayed:
+                    hand_on(part, step).start()
+
+    def parts_of(half):
+        return range(half * LANES // PART, (half + 1) * LANES // PART)
+
     gains = skip[...]
     for half in range(2):
         over_chips(lambda dy, dz: backward(half, dy, dz, seat(-dy, -dz)).wait_recv())
+        if half:
+            end_near(0)
         span = slice(half * LANES, (half + 1) * LANES)
         blocks = returned[half].astype(F32)
         conv_out = blocks[:, :GROUP].reshape(width, LANES).T
@@ -323,11 +378,13 @@
         positions = me * tokens + half * LANES + lax.broadcasted_iota(jnp.int32, (LANES, width), 0)
         grad_out = jnp.where(positions >= suffix_start[0], cotangent[span, :].astype(F32), 0.0)
         grad_mixed = corr_out + gains * (grad_out * query[span, :].astype(F32))
-        grads[half, :, :width] = (grad_out * (conv_out + gains * (keys * values))).astype(BF16)
-        grads[half, :, width : 2 * width] = (grad_mixed * values).astype(BF16)
-        grads[half, :, 2 * width :] = (grad_mixed * keys).astype(BF16)
-        for step in range(1, columns):
-            gather(half, step).start()
+        pieces = (grad_out * (conv_out + gains * (keys * values)), grad_mixed * values, grad_mixed * keys)
+        pieces = jnp.concatenate(pieces, axis=1).astype(BF16)
+        for index, part in enumerate(parts_of(half)):
+            grads[part] = pieces[index * PART : (index + 1) * PART]
+            for step in near:
+                gather(part, step).start()
+    lend_input().start()
 
     for step in range(1, rings):
         along_ring(step, lax.rem(y - step + rings, rings)).wait_recv()
@@ -341,86 +398,116 @@
         device_id_type=MESH,
     )
     give_core.start()
+
+    def exchange(part):
+        return pltpu.make_async_remote_copy(
+            src_ref=partial.at[part],
+            dst_ref=arrived.at[part],
+            send_sem=part_send_sem.at[part],
+            recv_sem=part_recv_sem.at[part],
+            device_id=other_side,
+            device_id_type=MESH,
+        )
+
+    def weight_at(step, weight):
+        return weight[lax.rem(column + step, columns)].reshape(3 * width, -1)
+
+    for half in range(2):
+        if half:
+            end_near(half)
+        else:
+            give_core.wait_recv()
+        rows = slice(parts_of(half)[0], parts_of(half)[-1] + 1)
+        other = dot(grads[rows].reshape(LANES, -1), weight_at(0, other_weight))
+        for step in near:
+            if half == 0 and not relayed:
+                for part in parts_of(half):
+                    gather(part, step).wait_recv()
+            other += dot(gathered[rows, step].reshape(LANES, -1), weight_at(step, other_weight))
+        others[half] = other
+        for index, part in enumerate(parts_of(half)):
+            span = slice(index * PART, (index + 1) * PART)
+            if relayed:
+                hand_on(part, 1).wait_recv()
+                hand_on(part, 3).wait_recv()
+                others[half, span] += dot(gathered[part, 2], weight_at(2, other_weight))
+            partial[part] = others[half, span].astype(BF16)
+            exchange(part).start()
+
     for index in range(14, len(loads)):
         loads[index].wait()
-    give_core.wait_recv()
-
-    def exchange(half):
-        return pltpu.make_async_remote_copy(
-            src_ref=partial.at[half],
-            dst_ref=arrived.at[half],
-            send_sem=part_send_sem.at[half],
-            recv_sem=part_recv_sem.at[half],
-            device_id=other_side,
-            device_id_type=MESH,
-        )
-
-    def product_of(half, step, weight):
-        left = grads[half] if step == 0 else gathered[half, step]
-        return dot(left, weight[lax.rem(column + step, columns)].reshape(3 * width, -1))
-
-    for half in range(2):
-        other = product_of(half, 0, other_weight)
-        own = product_of(half, 0, own_weight)
+    for half in range(2):
+        rows = slice(parts_of(half)[0], parts_of(half)[-1] + 1)
+        own = dot(grads[rows].reshape(LANES, -1), weight_at(0, own_weight))
         for step in range(1, columns):
-            gather(half, step).wait_recv()
-            other += product_of(half, step, other_weight)
-        partial[half] = other.astype(BF16)
-        exchange(half).start()
-        for step in range(1, columns):
-            own += product_of(half, step, own_weight)
+            own += dot(gathered[rows, step].reshape(LANES, -1), weight_at(step, own_weight))
         totals[half] = own
 
-    parts = []
-    for half in range(2):
-        span = slice(half * LANES, (half + 1) * LANES)
-        exchange(half).wait_recv()
-        full_grad = totals[half] + arrived[half].astype(F32)
-        input_grad[span, :] = full_grad.astype(BF16)
-        weighted = full_grad * layer_input[span, :].astype(F32)
+    def tell(half, step, index):
+        return pltpu.make_async_remote_copy(
+            src_ref=scores.at[index, half],
+            dst_ref=scores.at[index, half],
+            send_sem=score_send_sem.at[half, step],
+            recv_sem=score_recv_sem.at[half, step],
+            device_id=along_ch(step),
+            device_id_type=MESH,
+        )
+
+    def share_scores(half, weighted):
         features = weighted.shape[1]
         folded = weighted[:, : min(LANES, features)]
         for start in range(LANES, features, LANES):
             folded = folded + weighted[:, start : start + LANES]
-        parts.append(jnp.sum(folded.T, axis=0, keepdims=True))
-    scores[lane] = jnp.broadcast_to(jnp.concatenate(parts, axis=1), (8, tokens))
-
-    def tell(step, index):
-        return pltpu.make_async_remote_copy(
-            src_ref=scores.at[index],
-            dst_ref=scores.at[index],
-            send_sem=score_send_sem.at[step],
-            recv_sem=score_recv_sem.at[step],
-            device_id=along_ch(step),
-            device_id_type=MESH,
-        )
-
-    for step in range(1, peers):
-        tell(step, lane).start()
+        scores[lane, half] = jnp.broadcast_to(jnp.sum(folded.T, axis=0, keepdims=True), (8, LANES))
+        for step in range(1, peers):
+            tell(half, step, lane).start()
+
+    def finish(half):
+        for part in parts_of(half):
+            exchange(part).wait_recv()
+        rows = slice(parts_of(half)[0], parts_of(half)[-1] + 1)
+        full_grad = totals[half] + arrived[rows].astype(F32).reshape(LANES, -1)
+        input_grad[half * LANES : (half + 1) * LANES, :] = full_grad.astype(BF16)
+        return full_grad
+
+    share_scores(0, finish(0) * layer_input[:LANES, :].astype(F32))
+    lend_input().wait_recv()
+    share_scores(
+        1, totals[1] * layer_input[LANES:, :].astype(F32) + others[1] * other_input[...].astype(F32)
+    )
+    finish(1)
 
     over_chips(lambda dy, dz: forward(dy, dz, chip).wait_send())
     give_share.wait_send()
     swap.wait_send()
     swap_back.wait_send()
     give_core.wait_send()
-    for step in range(1, line):
-        along_line(step, z).wait_send()
+    if half_line:
+        along_line(0, 0, z).wait_send()
+    for step, block in within:
+        along_line(step, block, z).wait_send()
     for step in range(1, rings):
         along_ring(step, y).wait_send()
     for half in range(2):
         over_chips(lambda dy, dz: backward(half, dy, dz, chip).wait_send())
-        for step in range(1, columns):
-            gather(half, step).wait_send()
-        exchange(half).wait_send()
-
-    for step in range(1, peers):
-        tell(step, lax.rem(lane - step + peers, peers)).wait_recv()
-    total = scores[0]
-    for index in range(1, peers):
-        total = total + scores[index]
-    attribution[...] = total[0:1, :]
-    for step in range(1, peers):
-        tell(step, lane).wait_send()
+        for part in parts_of(half):
+            for step in near:
+                gather(part, step).wait_send()
+                if relayed:
+                    hand_on(part, step).wait_send()
+            exchange(part).wait_send()
+    lend_input().wait_send()
+
+    for half in range(2):
+        for step in range(1, peers):
+            tell(half, step, lax.rem(lane - step + peers, peers)).wait_recv()
+        total = scores[0, half]
+        for index in range(1, peers):
+            total = total + scores[index, half]
+        attribution[:, half * LANES : (half + 1) * LANES] = total[0:1, :]
+    for half in range(2):
+        for step in range(1, peers):
+            tell(half, step, lane).wait_send()
 
 
 def shards(query, key_proj, value, filt, skip, cotangent, suffix_start, layer_input, in_weight):
@@ -432,6 +519,7 @@
     rings = chips // line
     tables = transform_tables(sources, tokens)
     count = GROUP * sources
+    parts = tokens // PART
     vmem = pl.BlockSpec(memory_space=pltpu.VMEM)
     smem = pl.BlockSpec(memory_space=pltpu.SMEM)
     hbm = pl.BlockSpec(memory_space=pl.ANY)
@@ -444,7 +532,8 @@
         in_specs=[hbm] * (7 + len(tables)) + [vmem, smem],
         out_specs=(vmem, vmem),
         scratch_shapes=[
-            block, block, block, pltpu.VMEM((tokens, width), F32), block, pltpu.VMEM((tokens, features), BF16),
+            block, block, block, pltpu.VMEM((tokens, width), F32), block,
+            pltpu.VMEM((tokens, features), BF16), pltpu.VMEM((LANES, features), BF16),
             weight_block, weight_block,
             *[pltpu.VMEM(table.shape, table.dtype) for table in tables],
             pltpu.VMEM((chips, 48, LANES), BF16),
@@ -460,17 +549,20 @@
             pltpu.VMEM((chips, 16, LANES), BF16),
             pltpu.VMEM((2, chips, 16, LANES), BF16),
             pltpu.VMEM((2, chips, 16, LANES), BF16),
-            pltpu.VMEM((2, LANES, 3 * width), BF16),
-            pltpu.VMEM((2, columns, LANES, 3 * width), BF16),
-            pltpu.VMEM((2, LANES, features), BF16),
-            pltpu.VMEM((2, LANES, features), BF16),
+            pltpu.VMEM((parts, PART, 3 * width), BF16),
+            pltpu.VMEM((parts, columns, PART, 3 * width), BF16),
+            pltpu.VMEM((parts, PART, features), BF16),
+            pltpu.VMEM((parts, PART, features), BF16),
             pltpu.VMEM((2, LANES, features), F32),
-            pltpu.VMEM((peers, 8, tokens), F32),
+            pltpu.VMEM((2, LANES, features), F32),
+            pltpu.VMEM((peers, 2, 8, LANES), F32),
             dma((15 + columns,)),
             dma((chips,)), dma((chips,)), dma((2,)),
             dma((2, chips)), dma((2, chips)), dma((2,)),
             dma((2,)), dma((line,)), dma((line,)), dma((rings,)), dma((rings,)), dma((2,)),
-            dma((2, columns)), dma((2, columns)), dma((2,)), dma((2,)), dma((peers,)), dma((peers,)),
+            dma((2,)),
+            dma((parts, columns)), dma((parts, columns)), dma((parts, 2)), dma((parts, 2)),
+            dma((parts,)), dma((parts,)), dma((2, peers)), dma((2, peers)),
         ],
         compiler_params=pltpu.CompilerParams(
             collective_id=0, has_side_effects=True, vmem_limit_bytes=56 * 1024 * 1024

time: 106 us -> 102 us (0.962)
  the two profiles are of different devices: /device:TPU:32 before, /device:TPU:136 now
where the time goes in v4:
time: 102 us
  Pallas kernels  98.2 us (96%)
  local copies, waits for them, and re-layouts  2.8 us (3%)
  between operations  1.29 us (1%)
    pallas_call x1, Pallas kernels, shards(): pl.pallas_call(functools.partial(kernel, chips, columns), out_shape=(jax....  98.2 us
    unnamed x2, local copies, waits for them, and re-layouts  2.8 us

profile of v4, /device:TPU:136, one launch (start us, length us, event | category | flops | bytes accessed | tf_op | source)
XLA Modules:
  0.0 102.3 jit_solution(5533417732844406494)
XLA Ops:
  1.3 98.2 %conv_backward.1 = (bf16[256,256]{1,0:T(8,128)(2,1)}, f32[1,256]{1,0:T(1,128)}) custom-call(bf16[256,256]{1,0:T(8,128)(2,1)} %query_hbm.1, bf16[256,256]{1,0:T(8,128)(2,1)} %key_hbm.1, bf16[256,256]{1,0:T(8,128)(2,1)} %value_hbm.1, f32[256,256]{1,0:T(8,128)} %filt_hbm.1, bf16[256,256]{1,0:T(8,128)(2,1)} %cotangent_hbm.1, bf16[256,256]{1,0:T(8,128)(2,1)} %input_hbm.1, ...), custom_call_target="tpu_custom_call" | custom-call | tf_op jit(solution)/shard_map/conv_backward/pallas_call | solution.py:529
  99.5 1.6 %copy.23 = bf16[256,256]{1,0:T(8,128)(2,1)} copy(bf16[256,256]{1,0:T(8,128)(2,1)} %get-tuple-element.8) | data formatting | bytes 262144
  101.0 1.2 %copy.24 = f32[256]{0:T(256)} copy(f32[256]{0:T(256)} %bitcast.4) | data formatting | bytes 2048

commit v5 on v4

--- a/solution.py
+++ b/solution.py
@@ -15,6 +15,7 @@
 GROUP = 8
 LINE = 8
 PART = 64
+EARLIEST = 4096
 
 
 def split_high_low(table):
@@ -118,10 +119,6 @@
     def greet(device):
         pl.semaphore_signal(barrier, inc=1, device_id=device, device_id_type=MESH)
 
-    for step in range(1, peers):
-        greet(along_ch(step))
-    over_chips(lambda dy, dz: greet(same_core(dy, dz)))
-    greet(other_core)
     loads = [
         (key_hbm, key_proj), (value_hbm, value), (filt_hbm, filt), (cotangent_hbm, cotangent), (query_hbm, query),
         (one_hbm, one), (cos_hbm, turn_cos), (sin_hbm, turn_sin), (two_hi_hbm, two_hi), (two_lo_hbm, two_lo),
@@ -130,7 +127,13 @@
     ]
     loads += [(weight_hbm.at[:, 2 * index + side], own_weight.at[index]) for index in range(columns)]
     loads = [pltpu.make_async_copy(a, b, load_sem.at[i]) for i, (a, b) in enumerate(loads)]
-    for load in loads:
+    for load in loads[:5]:
+        load.start()
+    for step in range(1, peers):
+        greet(along_ch(step))
+    over_chips(lambda dy, dz: greet(same_core(dy, dz)))
+    greet(other_core)
+    for load in loads[5:]:
         load.start()
 
     loads[0].wait()
@@ -146,15 +149,60 @@
 
     pl.semaphore_wait(barrier, chips + peers - 1)
 
-    def forward(dy, dz, index):
-        return pltpu.make_async_remote_copy(
-            src_ref=send.at[seat(dy, dz)],
-            dst_ref=recv.at[core, index],
-            send_sem=send_sem.at[dy * line + dz],
-            recv_sem=recv_sem.at[dy * line + dz],
+    quiet = EARLIEST // (2 * tokens)
+    is_quiet = chip < quiet
+    rest = chips - quiet
+
+    def forward(dy, dz, short):
+        rows = pl.ds(0, 32 if short else 48)
+        return pltpu.make_async_remote_copy(
+            src_ref=send.at[seat(dy, dz), rows],
+            dst_ref=recv.at[core, chip, rows],
+            send_sem=send_sem.at[0],
+            recv_sem=recv_sem.at[int(short)],
             device_id=same_core(dy, dz),
             device_id_type=MESH,
         )
+
+    def send_signals():
+        if quiet:
+            @pl.when(is_quiet)
+            def _():
+                over_chips(lambda dy, dz: forward(dy, dz, True).start())
+
+        @pl.when(jnp.logical_not(is_quiet))
+        def _():
+            over_chips(lambda dy, dz: forward(dy, dz, False).start())
+
+    def drain(place, semaphore):
+        pltpu.make_async_copy(place, place, semaphore).wait()
+
+    def receive_signals(full, short):
+        if full:
+            drain(recv.at[core, pl.ds(0, full)], recv_sem.at[0])
+        if short:
+            drain(recv.at[core, pl.ds(0, short), pl.ds(0, 32)], recv_sem.at[1])
+
+    def end_signals():
+        if quiet:
+            @pl.when(is_quiet)
+            def _():
+                receive_signals(rest, quiet - 1)
+
+        @pl.when(jnp.logical_not(is_quiet))
+        def _():
+            receive_signals(rest - 1, quiet)
+
+    def end_sends():
+        if quiet and chips > 1:
+            @pl.when(is_quiet)
+            def _():
+                drain(send.at[pl.ds(0, chips - 1), pl.ds(0, 32)], send_sem.at[0])
+
+        @pl.when(jnp.logical_not(is_quiet))
+        def _():
+            if chips > 1:
+                drain(send.at[pl.ds(0, chips - 1)], send_sem.at[0])
 
     per_column = sources // columns
     share_rows = width // per_column
@@ -173,7 +221,9 @@
         device_id_type=MESH,
     )
     give_share.start()
-    over_chips(lambda dy, dz: forward(dy, dz, chip).start())
+    send_signals()
+    if quiet:
+        recv[core, 0:quiet, 32:48, :] = jnp.zeros((quiet, 16, LANES), BF16)
     recv[core, chip] = send[chip]
 
     def mirror(index, distance):
@@ -203,7 +253,7 @@
     give_share.wait_recv()
     if half_line:
         along_line(0, 0, z).start()
-    over_chips(lambda dy, dz: forward(dy, dz, seat(-dy, -dz)).wait_recv())
+    end_signals()
 
     theirs = pl.ds(pl.multiple_of(16 * (1 - core), 16), 32)
     swap = pltpu.make_async_remote_copy(
@@ -217,10 +267,6 @@
     swap.start()
 
     swap.wait_recv()
-    if half_line:
-        along_line(0, 0, mirror(z)).wait_recv()
-    for step, block in within:
-        along_line(step, block, z).start()
 
     def lend_input():
         place = pl.ds(LANES, LANES)
@@ -257,6 +303,10 @@
             spec_hi[place, span], spec_lo[place, span] = halves(real * cos + imag * sin)
             span = slice(tokens + half * LANES, tokens + (half + 1) * LANES)
             spec_hi[place, span], spec_lo[place, span] = halves(imag * cos - real * sin)
+    if half_line:
+        along_line(0, 0, mirror(z)).wait_recv()
+    for step, block in within:
+        along_line(step, block, z).start()
     spec[...] = (
         dot(spec_hi[...], two_hi[...]) + dot(spec_lo[...], two_hi[...]) + dot(spec_hi[...], two_lo[...])
     )
@@ -303,10 +353,6 @@
             device_id_type=MESH,
         )
 
-    for step, block in within:
-        along_line(step, block, ahead(-step)).wait_recv()
-    for step in range(1, rings):
-        along_ring(step, y).start()
     mine = results[core].astype(F32)
     swap_back.wait_recv()
     given = swapped[...].astype(F32)
@@ -316,19 +362,32 @@
         span = slice(half * GROUP, (half + 1) * GROUP)
         outgoing[half] = jnp.concatenate([conv[:, span], corr[:, span]], axis=1).astype(BF16)
 
-    def backward(half, dy, dz, index):
+    def backward(half, dy, dz):
         return pltpu.make_async_remote_copy(
             src_ref=outgoing.at[half, seat(dy, dz)],
-            dst_ref=returned.at[half, index],
-            send_sem=send_back_sem.at[half, dy * line + dz],
-            recv_sem=recv_back_sem.at[half, dy * line + dz],
+            dst_ref=returned.at[half, chip],
+            send_sem=send_back_sem.at[half],
+            recv_sem=recv_back_sem.at[half],
             device_id=same_core(dy, dz),
             device_id_type=MESH,
         )
 
     for half in range(2):
-        over_chips(lambda dy, dz: backward(half, dy, dz, chip).start())
+        over_chips(lambda dy, dz: backward(half, dy, dz).start())
         returned[half, chip] = outgoing[half, chip]
+
+    for step, block in within:
+        along_line(step, block, ahead(-step)).wait_recv()
+    for step in range(1, rings):
+        along_ring(step, y).start()
+    end_sends()
+    give_share.wait_send()
+    swap.wait_send()
+    swap_back.wait_send()
+    if half_line:
+        along_line(0, 0, z).wait_send()
+    for step, block in within:
+        along_line(step, block, z).wait_send()
 
     def gather(part, step):
         return pltpu.make_async_remote_copy(
@@ -366,7 +425,8 @@
 
     gains = skip[...]
     for half in range(2):
-        over_chips(lambda dy, dz: backward(half, dy, dz, seat(-dy, -dz)).wait_recv())
+        if chips > 1:
+            drain(returned.at[half, pl.ds(0, chips - 1)], recv_back_sem.at[half])
         if half:
             end_near(0)
         span = slice(half * LANES, (half + 1) * LANES)
@@ -470,33 +530,27 @@
         input_grad[half * LANES : (half + 1) * LANES, :] = full_grad.astype(BF16)
         return full_grad
 
-    share_scores(0, finish(0) * layer_input[:LANES, :].astype(F32))
-    lend_input().wait_recv()
-    share_scores(
-        1, totals[1] * layer_input[LANES:, :].astype(F32) + others[1] * other_input[...].astype(F32)
-    )
-    finish(1)
-
-    over_chips(lambda dy, dz: forward(dy, dz, chip).wait_send())
-    give_share.wait_send()
-    swap.wait_send()
-    swap_back.wait_send()
     give_core.wait_send()
-    if half_line:
-        along_line(0, 0, z).wait_send()
-    for step, block in within:
-        along_line(step, block, z).wait_send()
     for step in range(1, rings):
         along_ring(step, y).wait_send()
     for half in range(2):
-        over_chips(lambda dy, dz: backward(half, dy, dz, chip).wait_send())
+        if chips > 1:
+            drain(outgoing.at[half, pl.ds(0, chips - 1)], send_back_sem.at[half])
         for part in parts_of(half):
             for step in near:
                 gather(part, step).wait_send()
                 if relayed:
                     hand_on(part, step).wait_send()
-            exchange(part).wait_send()
+
+    share_scores(0, finish(0) * layer_input[:LANES, :].astype(F32))
+    lend_input().wait_recv()
+    share_scores(
+        1, totals[1] * layer_input[LANES:, :].astype(F32) + others[1] * other_input[...].astype(F32)
+    )
+    finish(1)
     lend_input().wait_send()
+    for part in range(tokens // PART):
+        exchange(part).wait_send()
 
     for half in range(2):
         for step in range(1, peers):
@@ -557,8 +611,8 @@
             pltpu.VMEM((2, LANES, features), F32),
             pltpu.VMEM((peers, 2, 8, LANES), F32),
             dma((15 + columns,)),
-            dma((chips,)), dma((chips,)), dma((2,)),
-            dma((2, chips)), dma((2, chips)), dma((2,)),
+            dma((1,)), dma((2,)), dma((2,)),
+            dma((2,)), dma((2,)), dma((2,)),
             dma((2,)), dma((line,)), dma((line,)), dma((rings,)), dma((rings,)), dma((2,)),
             dma((2,)),
             dma((parts, columns)), dma((parts, columns)), dma((parts, 2)), dma((parts, 2)),

time: 102 us -> 99.1 us (0.972)
  the two profiles are of different devices: /device:TPU:136 before, /device:TPU:128 now
where the time goes in v5:
time: 99.1 us; the launch traced here: 98.9 us
  Pallas kernels  94.8 us (96%)
  local copies, waits for them, and re-layouts  2.8 us (3%)
  between operations  1.29 us (1%)
    pallas_call x1, Pallas kernels, shards(): pl.pallas_call(functools.partial(kernel, chips, columns), out_shape=(jax....  94.8 us
    unnamed x2, local copies, waits for them, and re-layouts  2.8 us

profile of v5, /device:TPU:128, one launch (start us, length us, event | category | flops | bytes accessed | tf_op | source)
XLA Modules:
  0.0 98.9 jit_solution(14354668635405003714)
XLA Ops:
  1.3 94.8 %conv_backward.1 = (bf16[256,256]{1,0:T(8,128)(2,1)}, f32[1,256]{1,0:T(1,128)}) custom-call(bf16[256,256]{1,0:T(8,128)(2,1)} %query_hbm.1, bf16[256,256]{1,0:T(8,128)(2,1)} %key_hbm.1, bf16[256,256]{1,0:T(8,128)(2,1)} %value_hbm.1, f32[256,256]{1,0:T(8,128)} %filt_hbm.1, bf16[256,256]{1,0:T(8,128)(2,1)} %cotangent_hbm.1, bf16[256,256]{1,0:T(8,128)(2,1)} %input_hbm.1, ...), custom_call_target="tpu_custom_call" | custom-call | tf_op jit(solution)/shard_map/conv_backward/pallas_call | solution.py:583
  96.1 1.6 %copy.23 = bf16[256,256]{1,0:T(8,128)(2,1)} copy(bf16[256,256]{1,0:T(8,128)(2,1)} %get-tuple-element.8) | data formatting | bytes 262144
  97.7 1.2 %copy.24 = f32[256]{0:T(256)} copy(f32[256]{0:T(256)} %bitcast.4) | data formatting | bytes 2048

commit v6 on v5

--- a/solution.py
+++ b/solution.py
@@ -250,10 +250,10 @@
     def ahead(step):
         return z // half_line * half_line + lax.rem(z + step + half_line, half_line)
 
+    end_signals()
     give_share.wait_recv()
     if half_line:
         along_line(0, 0, z).start()
-    end_signals()
 
     theirs = pl.ds(pl.multiple_of(16 * (1 - core), 16), 32)
     swap = pltpu.make_async_remote_copy(

time: 99.1 us -> 98.4 us (level)
  the two profiles are of different devices: /device:TPU:128 before, /device:TPU:96 now
where the time goes in v6:
time: 98.4 us; the launch traced here: 98.2 us
  Pallas kernels  94.1 us (96%)
  local copies, waits for them, and re-layouts  2.8 us (3%)
  between operations  1.29 us (1%)
    pallas_call x1, Pallas kernels, shards(): pl.pallas_call(functools.partial(kernel, chips, columns), out_shape=(jax....  94.1 us
    unnamed x2, local copies, waits for them, and re-layouts  2.8 us

profile of v6, /device:TPU:96, one launch (start us, length us, event | category | flops | bytes accessed | tf_op | source)
XLA Modules:
  0.0 98.2 jit_solution(1082992249750693459)
XLA Ops:
  1.3 94.1 %conv_backward.1 = (bf16[256,256]{1,0:T(8,128)(2,1)}, f32[1,256]{1,0:T(1,128)}) custom-call(bf16[256,256]{1,0:T(8,128)(2,1)} %query_hbm.1, bf16[256,256]{1,0:T(8,128)(2,1)} %key_hbm.1, bf16[256,256]{1,0:T(8,128)(2,1)} %value_hbm.1, f32[256,256]{1,0:T(8,128)} %filt_hbm.1, bf16[256,256]{1,0:T(8,128)(2,1)} %cotangent_hbm.1, bf16[256,256]{1,0:T(8,128)(2,1)} %input_hbm.1, ...), custom_call_target="tpu_custom_call" | custom-call | tf_op jit(solution)/shard_map/conv_backward/pallas_call | solution.py:583
  95.4 1.6 %copy.23 = bf16[256,256]{1,0:T(8,128)(2,1)} copy(bf16[256,256]{1,0:T(8,128)(2,1)} %get-tuple-element.8) | data formatting | bytes 262144
  96.9 1.2 %copy.24 = f32[256]{0:T(256)} copy(f32[256]{0:T(256)} %bitcast.4) | data formatting | bytes 2048
